TPU v7x, 32 devices: a whole 2x2x4 slice. The times are simulated.
32 devices in a mesh: seq: 8 (over z, y), row: 4 (over x, core).
Axes of the slice: x: 2, y: 2, z: 4, core: 2. Of those that a mesh axis runs over, the one named last changes fastest.
Arguments:
- tokens: bfloat16 [4, 5120, 512], P('row', 'seq'), may hold values from -6 to 6
- cotangent: bfloat16 [4, 5120, 512], P('row', 'seq'), may hold values from -6 to 6
- w_query: bfloat16 [512, 512], replicated, may hold values from -0.25 to 0.25
- w_kv: bfloat16 [512, 128], replicated, may hold values from -0.25 to 0.25
- w_route: bfloat16 [512, 8], replicated, may hold values from -0.5 to 0.5
- w_out: bfloat16 [512, 512], replicated, may hold values from -20 to 20
- w_up: bfloat16 [512, 2048], replicated, may hold values from -0.25 to 0.25
- bias_up: float32 [2048], replicated, may hold values from -3 to 3
- w_down: bfloat16 [2048, 512], replicated, may hold values from -0.125 to 0.125
- bias_down: float32 [512], replicated, may hold values from -4 to 4
- gain_one: float32 [512], replicated, may hold values from 0.5 to 1.5
- shift_one: float32 [512], replicated, may hold values from -0.15625 to 0.15625
- gain_two: float32 [512], replicated, may hold values from 0.5 to 1.5
- shift_two: float32 [512], replicated, may hold values from -3 to 3
- choices: int32 [4, 5120, 2], P('row', 'seq'), may hold values from 0 to 7, all different within a row
- segment_ids: int32 [4, 5120], P('row', 'seq'), may hold values from 0 to 3, as said below
Outputs:
- layer_out: bfloat16 [4, 5120, 512], P('row', 'seq')
- grad_tokens: float32 [4, 5120, 512], P('row', 'seq')
- grad_query: float32 [512, 512], replicated
- grad_kv: float32 [512, 128], replicated
- grad_route: float32 [512, 8], replicated
- grad_out: float32 [512, 512], replicated
- grad_up: float32 [512, 2048], replicated
- grad_bias_up: float32 [2048], replicated
- grad_down: float32 [2048, 512], replicated
- grad_bias_down: float32 [512], replicated
- grad_gain_one: float32 [512], replicated
- grad_shift_one: float32 [512], replicated
- grad_gain_two: float32 [512], replicated
- grad_shift_two: float32 [512], replicated
Inputs may be any that keep to these rules, and one draw needn't show every extreme that they name: For each token, its two experts choices[t, 0] and choices[t, 1] differ; different tokens may name the same experts, and every expert is named by some token. `segment_ids`: each row holds 4 documents as contiguous runs, numbered 0 to 3 in order along the row, every one present, of uneven lengths; tokens attend to tokens of their own row with the same id.
All inputs are finite; a program needn't handle non-finite values.
Results may differ from a plain program's by a relative error of at most 0.015.
Values may be sent and summed in bfloat16 or wider, within the bound.
No kernel may reach another device: no remote copies, remote signals or barrier semaphores. Data moves between devices by JAX's collectives and lax.ppermute only.
A program may use at most 128 MiB of HBM per device.

v0:
```python
import math

import jax
import jax.numpy as jnp
from jax import lax
from jax.sharding import PartitionSpec as P

epsilon = 1e-05
highest = lax.Precision.HIGHEST


def normalize(values_in, gain, shift):
    row_mean = jnp.mean(values_in, axis=-1, keepdims=True)
    centred = values_in - row_mean
    inverse = lax.rsqrt(jnp.mean(centred * centred, axis=-1, keepdims=True) + epsilon)
    unit_rows = centred * inverse
    return (unit_rows * gain + shift, unit_rows, inverse)


def normalize_back(upstream, unit_rows, inverse, gain):
    scaled = upstream * gain
    inner_part = (
        scaled
        - jnp.mean(scaled, axis=-1, keepdims=True)
        - unit_rows * jnp.mean(scaled * unit_rows, axis=-1, keepdims=True)
    )
    return (inverse * inner_part, jnp.sum(upstream * unit_rows, axis=0), jnp.sum(upstream, axis=0))


def inner_rows(left, right):
    return lax.dot_general(
        left, right, (((0,), (0,)), ((), ())), preferred_element_type=jnp.float32
    )


def outer_cols(left, right):
    return lax.dot_general(
        left, right, (((1,), (1,)), ((), ())), preferred_element_type=jnp.float32
    )


def block_plan(rows_total, rows_here):
    block_rows = math.gcd(rows_total, rows_here)
    return (block_rows, rows_total // block_rows)


def over_blocks(update, state, key_part, seg_part, rows_here):
    block_rows, block_count = block_plan(key_part.shape[0], rows_here)
    key_blocks = key_part.reshape(block_count, block_rows, key_part.shape[1])
    seg_blocks = seg_part.reshape(block_count, block_rows)
    offsets = block_rows * jnp.arange(block_count, dtype=jnp.int32)

    def scan_step(inner_state, pieces):
        return (update(inner_state, pieces[0], pieces[1], pieces[2]), None)

    state, _ = lax.scan(scan_step, state, (key_blocks, seg_blocks, offsets))
    return state


def key_scores(queries, seg_query, key_part, seg_part):
    head_size = queries.shape[-1]
    scores = head_size ** (-0.5) * jnp.einsum(
        "jtd,kd->jtk", queries, key_part[:, :head_size], preferred_element_type=jnp.float32
    )
    allowed = seg_query[None, :, None] == seg_part[None, None, :]
    return (scores, allowed)


def forward_update(queries, seg_query):
    head_size = queries.shape[-1]

    def update(state, key_part, seg_part, first_row):
        maxima, totals, accumulated = state
        scores, allowed = key_scores(queries, seg_query, key_part, seg_part)
        scores = jnp.where(allowed, scores, -1e30)
        new_maxima = jnp.maximum(maxima, jnp.max(scores, axis=-1))
        weights = jnp.where(allowed, jnp.exp(scores - new_maxima[..., None]), 0.0)
        factor = jnp.exp(maxima - new_maxima)
        totals = totals * factor + jnp.sum(weights, axis=-1)
        accumulated = accumulated * factor[..., None] + jnp.einsum(
            "jtk,kd->jtd",
            weights.astype(jnp.bfloat16),
            key_part[:, head_size:],
            preferred_element_type=jnp.float32,
        )
        return (new_maxima, totals, accumulated)

    return update


def backward_terms(queries, seg_query, grad_heads, log_total, row_delta, key_part, seg_part):
    head_size = queries.shape[-1]
    scores, allowed = key_scores(queries, seg_query, key_part, seg_part)
    probability = jnp.where(allowed, jnp.exp(scores - log_total[..., None]), 0.0)
    grad_prob = jnp.einsum(
        "jtd,kd->jtk", grad_heads, key_part[:, head_size:], preferred_element_type=jnp.float32
    )
    grad_scores = (probability * (grad_prob - row_delta[..., None])).astype(jnp.bfloat16)
    scaling = head_size ** (-0.5)
    grad_query = scaling * jnp.einsum(
        "jtk,kd->jtd", grad_scores, key_part[:, :head_size], preferred_element_type=jnp.float32
    )
    grad_keys = scaling * jnp.einsum(
        "jtk,jtd->kd", grad_scores, queries, preferred_element_type=jnp.float32
    )
    grad_values = jnp.einsum(
        "jtk,jtd->kd",
        probability.astype(jnp.bfloat16),
        grad_heads,
        preferred_element_type=jnp.float32,
    )
    return (grad_query, jnp.concatenate([grad_keys, grad_values], axis=1))


def summed_update(queries, seg_query, grad_heads, log_total, row_delta):

    def update(state, key_part, seg_part, first_row):
        grad_query, buffer = state
        term_query, term_keys = backward_terms(
            queries, seg_query, grad_heads, log_total, row_delta, key_part, seg_part
        )
        current = lax.dynamic_slice_in_dim(buffer, first_row, key_part.shape[0], 0)
        buffer = lax.dynamic_update_slice_in_dim(buffer, current + term_keys, first_row, 0)
        return (grad_query + term_query, buffer)

    return update


def local(
    tokens,
    cotangent,
    w_query,
    w_kv,
    w_route,
    w_out,
    w_up,
    bias_up,
    w_down,
    bias_down,
    gain_one,
    shift_one,
    gain_two,
    shift_two,
    choices,
    segment_ids,
):
    inputs_f = tokens[0].astype(jnp.float32)
    rows_here = inputs_f.shape[0]
    experts = w_route.shape[1]
    head_size = w_kv.shape[1] // 2
    seg_query = segment_ids[0].astype(jnp.bfloat16)
    onehot = (choices[0][:, :, None] == jnp.arange(experts, dtype=jnp.int32)[None, None, :]).astype(
        jnp.float32
    )
    normed_one, unit_one, inverse_one = normalize(inputs_f, gain_one, shift_one)
    normed_low = normed_one.astype(jnp.bfloat16)
    query_all = jnp.dot(normed_low, w_query, preferred_element_type=jnp.float32)
    keys_values = jnp.dot(normed_low, w_kv, preferred_element_type=jnp.float32).astype(jnp.bfloat16)
    logits = jnp.dot(normed_low, w_route, preferred_element_type=jnp.float32)
    picked = jnp.einsum("tje,te->tj", onehot, logits, precision=highest)
    gate_weights = jax.nn.softmax(picked, axis=-1)
    queries = jnp.einsum(
        "tje,ted->jtd", onehot, query_all.reshape(rows_here, experts, head_size), precision=highest
    ).astype(jnp.bfloat16)
    initial = (
        jnp.full((2, rows_here), -1e30, jnp.float32),
        jnp.zeros((2, rows_here), jnp.float32),
        jnp.zeros((2, rows_here, head_size), jnp.float32),
    )
    update_fwd = forward_update(queries, seg_query)
    shard_part = (
        lax.all_gather(keys_values, "seq", axis=0, tiled=True),
        lax.all_gather(seg_query, "seq", axis=0, tiled=True),
    )
    maxima, totals, accumulated = over_blocks(
        update_fwd, initial, shard_part[0], shard_part[1], rows_here
    )
    head_outputs = accumulated / totals[..., None]
    log_total = maxima + jnp.log(totals)
    mixed = (
        jnp.einsum("tje,tj,jtd->ted", onehot, gate_weights, head_outputs, precision=highest)
        .reshape(rows_here, experts * head_size)
        .astype(jnp.bfloat16)
    )
    middle = inputs_f + jnp.dot(mixed, w_out, preferred_element_type=jnp.float32)
    normed_two, unit_two, inverse_two = normalize(middle, gain_two, shift_two)
    second = normed_two.astype(jnp.bfloat16)
    pre_activation = jnp.dot(second, w_up, preferred_element_type=jnp.float32) + bias_up
    activated, gelu_back = jax.vjp(
        lambda value_in: jax.nn.gelu(value_in, approximate=True), pre_activation
    )
    act_low = activated.astype(jnp.bfloat16)
    layer_output = middle + jnp.dot(act_low, w_down, preferred_element_type=jnp.float32) + bias_down
    grad_low = cotangent[0]
    grad_final = grad_low.astype(jnp.float32)
    grad_bias_down = jnp.sum(grad_final, axis=0)
    grad_down = inner_rows(act_low, grad_low)
    grad_act = outer_cols(grad_low, w_down)
    grad_pre = gelu_back(grad_act)[0].astype(jnp.bfloat16)
    grad_bias_up = jnp.sum(grad_pre.astype(jnp.float32), axis=0)
    grad_up = inner_rows(second, grad_pre)
    back_two, grad_gain_two, grad_shift_two = normalize_back(
        outer_cols(grad_pre, w_up), unit_two, inverse_two, gain_two
    )
    grad_middle = grad_final + back_two
    middle_low = grad_middle.astype(jnp.bfloat16)
    grad_out = inner_rows(mixed, middle_low)
    grad_mixed = outer_cols(middle_low, w_out).reshape(rows_here, experts, head_size)
    grad_slots = jnp.einsum("tje,ted->jtd", onehot, grad_mixed, precision=highest)
    grad_gates = jnp.sum(grad_slots * head_outputs, axis=-1).T
    grad_heads = (grad_slots * gate_weights.T[..., None]).astype(jnp.bfloat16)
    row_delta = jnp.sum(grad_heads.astype(jnp.float32) * head_outputs, axis=-1)
    grad_picked = gate_weights * (
        grad_gates - jnp.sum(gate_weights * grad_gates, axis=-1, keepdims=True)
    )
    grad_logits = jnp.einsum("tj,tje->te", grad_picked, onehot, precision=highest).astype(
        jnp.bfloat16
    )
    zeros_query = jnp.zeros((2, rows_here, head_size), jnp.float32)
    row_length = rows_here * lax.axis_size("seq")
    update_back = summed_update(queries, seg_query, grad_heads, log_total, row_delta)
    start_state = (zeros_query, jnp.zeros((row_length, 2 * head_size), jnp.float32))
    shard_part = (
        lax.all_gather(keys_values, "seq", axis=0, tiled=True),
        lax.all_gather(seg_query, "seq", axis=0, tiled=True),
    )
    grad_query_heads, buffer = over_blocks(
        update_back, start_state, shard_part[0], shard_part[1], rows_here
    )
    key_grads = lax.psum_scatter(buffer, "seq", scatter_dimension=0, tiled=True)
    grad_kv_low = key_grads.astype(jnp.bfloat16)
    grad_query_all = (
        jnp.einsum("tje,jtd->ted", onehot, grad_query_heads, precision=highest)
        .reshape(rows_here, experts * head_size)
        .astype(jnp.bfloat16)
    )
    grad_query = inner_rows(normed_low, grad_query_all)
    grad_kv = inner_rows(normed_low, grad_kv_low)
    grad_route = inner_rows(normed_low, grad_logits)
    grad_first = (
        outer_cols(grad_query_all, w_query)
        + outer_cols(grad_kv_low, w_kv)
        + outer_cols(grad_logits, w_route)
    )
    back_one, grad_gain_one, grad_shift_one = normalize_back(
        grad_first, unit_one, inverse_one, gain_one
    )
    grad_tokens = grad_middle + back_one
    reduced = lax.psum(
        (
            grad_query,
            grad_kv,
            grad_route,
            grad_out,
            grad_up,
            grad_bias_up,
            grad_down,
            grad_bias_down,
            grad_gain_one,
            grad_shift_one,
            grad_gain_two,
            grad_shift_two,
        ),
        ("seq", "row"),
    )
    return (layer_output.astype(jnp.bfloat16)[None], grad_tokens[None]) + tuple(reduced)


def solution(mesh):
    placed = (
        P("row", "seq", None),
        P("row", "seq", None),
        P(),
        P(),
        P(),
        P(),
        P(),
        P(),
        P(),
        P(),
        P(),
        P(),
        P(),
        P(),
        P("row", "seq", None),
        P("row", "seq"),
    )
    return jax.shard_map(
        local,
        mesh=mesh,
        in_specs=placed,
        out_specs=(
            P("row", "seq", None),
            P("row", "seq", None),
            P(),
            P(),
            P(),
            P(),
            P(),
            P(),
            P(),
            P(),
            P(),
            P(),
            P(),
            P(),
        ),
        check_vma=False,
    )
```

profile of v0, /device:TPU:0, one launch (start us, length us, event | category | flops | bytes accessed | tf_op | source)
XLA Modules:
  0.0 670.0 jit_solution(7895077907982227957)
XLA Ops:
  11.5 32.1 %all-gather = bf16[1,5120]{1,0:T(2,128)(2,1)S(1)} all-gather(bf16[1,640]{1,0:T(2,128)(2,1)S(1)} %convert_element_type.91), channel_id=2, replica_groups=mesh['seq'=8,'row'=4] {'seq'}, dimensions={1}, use_global_device_ids=true | all-gather | bytes 11520 | tf_op jit(solution)/shard_map/all_gather | solution.py:173
  50.9 4.8 fusion.60
  60.4 4.1 fusion.73
  68.9 69.1 %while.28 = (s32[]{:T(128)}, f32[2,640]{1,0:T(2,128)S(1)}, f32[2,640]{1,0:T(2,128)S(1)}, f32[2,640,64]{1,2,0:T(8,128)}, bf16[640]{0:T(1024)(128)(2,1)S(1)}, /*in...) while((s32[]{:T(128)}, f32[2,640]{1,0:T(2,128)S(1)}, ...), condition=%wide.region_7.8_spmd.clone, body=%wide.region_4.7_spmd.clone.sunk | while | flops 221026560 | bytes 28595412 | solution.py:56
  143.1 6.4 convolution_convert_fusion.1
  157.1 5.4 convert_reduce_fusion
  179.7 14.8 %multiply_reduce_fusion.6 = (f32[2,640]{0,1:T(8,128)}, f32[2,640]{0,1:T(8,128)}, bf16[2,640,64]{2,0,1:T(2,128)(2,1)}) fusion(f32[2,640,64]{2,0,1:T(2,128)} %copy-done.26, f32[2,640]{0,1:T(8,128)} %fusion.98, f32[640,8,64]{2,1,0:T(8,128)} %copy.98, s32[640,2]{1,0:T(8,128)S(1)} %copy-done.32), kind=kOutput, calls=%fused_computation.108 | convolution fusion | flops 8445440 | bytes 1822720 | tf_op jit(solution)/shard_map/tje,ted->jtd/dot_general | solution.py:209
  199.2 155.3 %while.29 = (s32[]{:T(128)}, f32[2,640,64]{1,2,0:T(8,128)}, f32[5120,128]{0,1:T(8,128)}, bf16[640]{0:T(1024)(128)(2,1)S(1)}, bf16[8,640]{1,0:T(8,128)(2,1)S(1)},...) while((s32[]{:T(128)}, f32[2,640,64]{1,2,0:T(8,128)}, ...), condition=%wide.region_14.15_spmd.clone, body=%wide.region_13.14_spmd.clone.sunk | while | flops 533340160 | bytes 42783044 | solution.py:56
  201.2 3.7 fusion.173
  220.6 3.7 fusion.173
  240.1 3.6 fusion.173
  259.7 3.7 fusion.173
  279.2 3.7 fusion.173
  298.7 3.6 fusion.173
  318.2 3.7 fusion.173
  337.7 3.6 fusion.173
  356.6 5.7 convolution_convert_fusion
  368.1 3.9 fusion.99
  372.0 4.7 fusion.61
  376.8 49.0 %reduce-scatter.2.cloned.1.call-done = f32[640,128]{0,1:T(8,128)} async-done(((f32[5120,128]{0,1:T(8,128)}), f32[640,128]{0,1:T(8,128)}) %reduce-scatter.2.cloned.1.call-update) | async-done | bytes 327696 | tf_op jit(solution)/shard_map/reduce_scatter | solution.py:230
  428.5 6.3 fusion.59
  439.9 4.3 fusion.72
  451.8 41.1 %all-reduce = (f32[512,8]{0,1:T(8,128)}, f32[2048]{0:T(1024)}, f32[512]{0:T(512)}, f32[512]{0:T(512)}, f32[512]{0:T(512)}, /*index=5*/f32[512]{0:T(512)}, f32[512]{0:T(512)}) all-reduce(f32[512,8]{0,1:T(8,128)S(1)} %fusion.89, f32[2048]{0:T(1024)S(1)} %copy-done.45, ...), channel_id=1, replica_groups=mesh['seq'=8,'row'=4] {'seq','row'}, use_global_device_ids=true, to_apply=%region_22.23 | all-reduce | flops 8704 | bytes 69632 | tf_op jit(solution)/shard_map/psum | solution.py:249
  492.9 159.3 %all-reduce.4.cloned.1.call-done = (f32[512,512]{1,0:T(8,128)}, f32[512,128]{1,0:T(8,128)}, f32[512,512]{1,0:T(8,128)}, f32[512,2048]{1,0:T(8,128)}, f32[2048,512]{1,0:T(8,128)}) async-done(((f32[512,512]{1,0:T(8,128)}, f32[512,128]{1,0:T(8,128)}, f32[512,512]{1,0:T(8,128)}, f32[512,2048]{1,0:T(8,128)}, f32[2048,512]{1,0:T(8,128)}), (f32[512,512]{1,0:T(8,128)}, f32[512,128]{1,0:T(8,128)}, ...) | async-done | bytes 10747920 | tf_op jit(solution)/shard_map/psum | solution.py:249
  (450 shorter events, 268.1 us)
Async XLA Ops:
  7.2 149.9 %copy-start = (bf16[2048,512]{1,0:T(8,128)(2,1)S(1)}, bf16[2048,512]{1,0:T(8,128)(2,1)}, u32[]{:S(2)}) copy-start(bf16[2048,512]{1,0:T(8,128)(2,1)} %param.28) | copy-start | bytes 6291460
  7.2 59.2 %all-gather.3.cloned.1.call-start = ((), (), s32[]{:S(2)}) async-start(), calls=%async_computation.1 | async-start | bytes 1474560 | tf_op jit(solution)/shard_map/all_gather | solution.py:172
  8.8 34.9 %copy-start.22 = (bf16[512,512]{1,0:T(8,128)(2,1)S(1)}, bf16[512,512]{1,0:T(8,128)(2,1)}, u32[]{:S(2)}) copy-start(bf16[512,512]{1,0:T(8,128)(2,1)} %param.22) | copy-start | bytes 1572868
  11.4 414.4 %reduce-scatter.2.cloned.1.call-start = ((), (), s32[]{:S(2)}) async-start(), calls=%async_computation.2 | async-start | bytes 2949120 | tf_op jit(solution)/shard_map/reduce_scatter | solution.py:230
  50.8 4.8 copy-start.31
  50.8 8.1 %copy-start.37 = (bf16[512,8]{0,1:T(8,128)(2,1)S(1)}, bf16[512,8]{0,1:T(8,128)(2,1)}, u32[]{:S(2)}) copy-start(bf16[512,8]{0,1:T(8,128)(2,1)} %param.24) | copy-start | bytes 24580
  64.5 4.4 copy-start.16
  157.1 5.4 copy-start.57
  194.5 4.7 copy-start.56
  200.8 4.0 copy-start.3
  220.2 4.0 copy-start.3
  239.7 4.0 copy-start.3
  259.3 4.0 copy-start.3
  278.8 4.0 copy-start.3
  298.3 4.0 copy-start.3
  317.8 4.0 copy-start.3
  337.3 4.0 copy-start.3
  354.6 297.5 %all-reduce.4.cloned.1.call-start = ((), (), s32[]{:S(2)}) async-start(), calls=%async_computation.3 | async-start | bytes 21495808 | tf_op jit(solution)/shard_map/psum | solution.py:249
  356.6 7.8 %copy-start.39 = (f32[512]{0:T(512)S(1)}, f32[512]{0:T(512)}, u32[]{:S(2)}) copy-start(f32[512]{0:T(512)} %param.30) | copy-start | bytes 6148
  356.6 7.8 %copy-start.48 = (f32[512]{0:T(512)S(1)}, f32[512]{0:T(512)}, u32[]{:S(2)}) copy-start(f32[512]{0:T(512)} %param.31) | copy-start | bytes 6148
  366.4 5.6 slice-start
  368.0 4.0 copy-start.28
  372.0 53.7 %copy-start.11 = (bf16[640,512]{0,1:T(8,128)(2,1)S(1)}, bf16[640,512]{0,1:T(8,128)(2,1)}, u32[]{:S(2)}) copy-start(bf16[640,512]{0,1:T(8,128)(2,1)} %copy-done.10) | copy-start | bytes 1966084
  652.2 5.4 copy-start.19
  (90 other events, 230.2 us)
Sparse Core Ops, SparseCore 0:
  11.5 44.7 all-gather.2
  354.7 70.9 reduce-scatter.1
  433.3 218.7 all-reduce.3
where the time goes:
time: 681 us; the launch traced here: 670 us
  waiting for transfers between devices  208 us (31%)
  matrix products  199 us (29%)
  local copies, waits for them, and re-layouts  105 us (15%)
  blocking collectives  73.2 us (11%)
  other arithmetic  53.2 us (8%)
  loops' own time  16.4 us (2%)
  between operations  14.6 us (2%)
    psum x1, waiting for transfers between devices, local(): lax.psum((grad_query, grad_kv, grad_route, grad_out, grad_up, grad_bias_u...  159 us
    reduce_scatter x1, waiting for transfers between devices, local(): key_grads = lax.psum_scatter(buffer, 'seq', scatter_dimension=0, tiled=True)  49 us
    psum x1, blocking collectives, local(): lax.psum((grad_query, grad_kv, grad_route, grad_out, grad_up, grad_bias_u...  41.1 us
    unnamed x124, local copies, waits for them, and re-layouts  34 us
    all_gather x1, blocking collectives, local(): lax.all_gather(seg_query, 'seq', axis=0, tiled=True)  32.1 us
    dot_general x8, matrix products, backward_terms(): jnp.einsum('jtd,kd->jtk', grad_heads, key_part[:, head_size:], preferred_...  29.2 us
    dot_general x8, matrix products, backward_terms(): jnp.einsum('jtk,jtd->kd', probability.astype(jnp.bfloat16), grad_heads, p...  29.2 us
    dynamic_update_slice x8, local copies, waits for them, and re-layouts, update(): lax.dynamic_update_slice_in_dim(buffer, current + term_keys, first_row, 0)  25.5 us
  transfers between devices with their start and end apart: 3, of which 2 were waited for; matrix products, arithmetic and copies ran while one was open for 10% of the time, Pallas kernels for 0%

commit v1 on v0

v1 whole, which is shorter than its diff:
```python
import functools

import jax
import jax.numpy as jnp
from jax import lax
from jax.experimental import pallas as pl
from jax.experimental.pallas import tpu as pltpu
from jax.sharding import PartitionSpec as P

f32 = jnp.float32
bf16 = jnp.bfloat16
epsilon = 1e-05
lanes = 128
half = 64
chunk = 128
pad_rows = 16
stat_rows = 80
masked = -2e30
lowest = -1e30
mib = 1 << 20


def nn(a, b):
    return lax.dot_general(a, b, (((1,), (0,)), ((), ())), preferred_element_type=f32)


def nt(a, b):
    return lax.dot_general(a, b, (((1,), (1,)), ((), ())), preferred_element_type=f32)


def tn(a, b):
    return lax.dot_general(a, b, (((0,), (0,)), ((), ())), preferred_element_type=f32)


def lane_ids(rows):
    return lax.broadcasted_iota(jnp.int32, (rows, lanes), 1)


def swap(values):
    return pltpu.roll(values, half, 1)


def column(row):
    return jnp.transpose(jnp.broadcast_to(row, (lanes, row.shape[1])), (1, 0))


def to_rows(row):
    count = row.shape[1] // lanes
    pieces = [row[:, i * lanes : (i + 1) * lanes] for i in range(count)]
    return jnp.concatenate(pieces + [jnp.zeros((8 - count, lanes), f32)], axis=0)


def from_rows(block, count):
    return jnp.concatenate([block[i : i + 1] for i in range(count)], axis=1)


def wide(values, count):
    return jnp.concatenate([values] * count, axis=1)


def normalized(x):
    centred = x - jnp.mean(x, axis=-1, keepdims=True)
    inverse = lax.rsqrt(jnp.mean(centred * centred, axis=-1, keepdims=True) + epsilon)
    return centred * inverse, inverse


def normalized_back(upstream, unit, inverse, gain):
    scaled = upstream * gain
    inner = (
        scaled
        - jnp.mean(scaled, axis=-1, keepdims=True)
        - unit * jnp.mean(scaled * unit, axis=-1, keepdims=True)
    )
    grad_gain = jnp.sum(upstream * unit, axis=0, keepdims=True)
    return inverse * inner, grad_gain, jnp.sum(upstream, axis=0, keepdims=True)


def project_kernel(tok, wq, wkv, wroute, gain, shift, choice, seg, kvm, qm, n_out, gates, picks):
    rows = tok.shape[0]
    unit, _ = normalized(tok[...].astype(f32))
    normed = (unit * gain[...] + shift[...]).astype(bf16)
    n_out[...] = normed
    ids = to_rows(seg[...].astype(f32))
    ids = jnp.concatenate([ids, jnp.zeros((pad_rows - 8, lanes), f32)], axis=0).astype(bf16)
    kvm[0:rows, :] = nn(normed, wkv[...]).astype(bf16)
    kvm[rows : rows + pad_rows, :] = ids
    qm[rows : rows + pad_rows, :] = ids
    first = column(choice[0:1, :].astype(f32)).astype(jnp.int32)
    second = column(choice[1:2, :].astype(f32)).astype(jnp.int32)
    picks[0] = first
    picks[1] = second
    lane = lane_ids(rows)
    low = lane < half
    query_all = nn(normed, wq[...])
    pairs = query_all.shape[1] // lanes
    one = jnp.zeros((rows, lanes), f32)
    two = jnp.zeros((rows, lanes), f32)
    for g in range(pairs):
        part = query_all[:, g * lanes : (g + 1) * lanes]
        one = jnp.where(first // 2 == g, part, one)
        two = jnp.where(second // 2 == g, part, two)
    one = jnp.where(first % 2 == 0, one, swap(one))
    two = jnp.where(second % 2 == 1, two, swap(two))
    scale = half ** (-0.5)
    qm[0:rows, :] = (jnp.where(low, one, two).astype(bf16).astype(f32) * scale).astype(bf16)
    logits = nt(normed, wroute[...])
    experts = logits.shape[1]
    slot = lax.broadcasted_iota(jnp.int32, (rows, experts), 1)
    picked_one = jnp.sum(jnp.where(slot == first[:, :experts], logits, 0.0), axis=1, keepdims=True)
    picked_two = jnp.sum(jnp.where(slot == second[:, :experts], logits, 0.0), axis=1, keepdims=True)
    top = jnp.maximum(picked_one, picked_two)
    exp_one = jnp.exp(picked_one - top)
    exp_two = jnp.exp(picked_two - top)
    gates[...] = jnp.where(low, exp_one, exp_two) / (exp_one + exp_two)


def id_range(message, rows):
    block = message[rows : rows + pad_rows, :][0:8].astype(f32)
    count = rows // lanes
    keep = lax.broadcasted_iota(jnp.int32, (8, lanes), 0) < count
    return jnp.min(jnp.where(keep, block, 1e9)), jnp.max(jnp.where(keep, block, -1e9))


def id_row(message, rows):
    block = message[rows : rows + pad_rows, :][0:8].astype(f32)
    return from_rows(block, rows // lanes)


def stack_slots(packed, place):
    low = lane_ids(packed.shape[0]) < half
    other = swap(packed.astype(f32)).astype(packed.dtype)
    zero = jnp.zeros_like(packed)
    if place == 0:
        return jnp.where(low, packed, zero), jnp.where(low, other, zero)
    return jnp.where(low, zero, other), jnp.where(low, zero, packed)


def store_stack(ref, packed, place):
    rows = packed.shape[0]
    one, two = stack_slots(packed, place)
    for c in range(rows // chunk):
        ref[2 * c * chunk : (2 * c + 1) * chunk, :] = one[c * chunk : (c + 1) * chunk]
        ref[(2 * c + 1) * chunk : (2 * c + 2) * chunk, :] = two[c * chunk : (c + 1) * chunk]


def over_pieces(parts, rows, own, visit):
    own_low, own_high = id_range(own, rows)
    for index, part in enumerate(parts):
        count = part.shape[0]

        def one(i, index=index, part=part):
            message = part.at[i]
            low, high = id_range(message, rows)
            meets = (low <= own_high) & (high >= own_low)
            uniform = (low == high) & (own_low == own_high) & meets

            @pl.when(uniform)
            def _():
                visit(index, i, message, True)

            @pl.when(meets & jnp.logical_not(uniform))
            def _():
                visit(index, i, message, False)

        if count == 1:
            one(0)
        else:
            pl.loop(0, count)(one)


def forward_kernel(piece_count, qm, own, *rest):
    parts = rest[:piece_count]
    heads, lse, stack, peak, total, seg = rest[piece_count:]
    rows = qm.shape[0] - pad_rows
    chunks = rows // chunk
    store_stack(stack, qm[0:rows, :], 0)
    peak[...] = jnp.full(peak.shape, lowest, f32)
    total[...] = jnp.zeros(total.shape, f32)
    seg[...] = column(id_row(own, rows))

    def visit(index, i, message, uniform):
        kv = message[0:rows, :]
        low = lane_ids(rows) < half
        values = jnp.where(low, jnp.ones_like(kv), kv)
        if not uniform:
            key_ids = id_row(message, rows)

        @pl.loop(0, chunks)
        def _(c):
            at = pl.ds(pl.multiple_of(c * 2 * chunk, 2 * chunk), 2 * chunk)
            scores = nt(stack[at, :], kv)
            if not uniform:
                mine = seg[pl.ds(pl.multiple_of(c * chunk, chunk), chunk), :]
                allowed = wide(jnp.concatenate([mine, mine], axis=0), rows // lanes) == key_ids
                scores = jnp.where(allowed, scores, masked)
            before = peak[at, :]
            now = jnp.maximum(before, jnp.max(scores, axis=1, keepdims=True))
            peak[at, :] = now
            weights = jnp.exp(scores - wide(now, rows // lanes)).astype(bf16)
            total[at, :] = total[at, :] * jnp.exp(before - now) + nn(weights, values)

    over_pieces(parts, rows, own, visit)
    low = lane_ids(chunk) < half
    for c in range(chunks):
        one = total[2 * c * chunk : (2 * c + 1) * chunk, :]
        two = total[(2 * c + 1) * chunk : (2 * c + 2) * chunk, :]
        one_other, two_other = swap(one), swap(two)
        heads[c * chunk : (c + 1) * chunk, :] = jnp.where(low, one_other, two) / jnp.where(
            low, one, two_other
        )
        for j, (whole, other) in enumerate(((one, one_other), (two, two_other))):
            at = slice((2 * c + j) * chunk, (2 * c + j + 1) * chunk)
            lse[at, :] = peak[at, :] + jnp.log(jnp.where(low, whole, other))


def query_back_kernel(
    piece_count, qm, dom, lse, delta, normed, picks, wq, dlog, wroute, own, *rest
):
    parts = rest[:piece_count]
    grad_wq, grad_n, stack, stack_do, total, seg = rest[piece_count:]
    rows = qm.shape[0] - pad_rows
    chunks = rows // chunk
    store_stack(stack, qm[0:rows, :], 0)
    store_stack(stack_do, dom[0:rows, :], 1)
    total[...] = jnp.zeros(total.shape, f32)
    seg[...] = column(id_row(own, rows))
    across = rows // lanes

    def visit(index, i, message, uniform):
        kv = message[0:rows, :]
        if not uniform:
            key_ids = id_row(message, rows)

        @pl.loop(0, chunks)
        def _(c):
            at = pl.ds(pl.multiple_of(c * 2 * chunk, 2 * chunk), 2 * chunk)
            scores = nt(stack[at, :], kv) - wide(lse[at, :], across)
            if not uniform:
                mine = seg[pl.ds(pl.multiple_of(c * chunk, chunk), chunk), :]
                allowed = wide(jnp.concatenate([mine, mine], axis=0), across) == key_ids
                scores = jnp.where(allowed, scores, masked)
            prob = jnp.exp(scores)
            grad_prob = nt(stack_do[at, :], kv) - wide(delta[at, :], across)
            total[at, :] += nn((prob * grad_prob).astype(bf16), kv)

    over_pieces(parts, rows, own, visit)
    low = lane_ids(rows) < half
    first = picks[0]
    second = picks[1]
    one = jnp.concatenate(
        [total[2 * c * chunk : (2 * c + 1) * chunk, :] for c in range(chunks)], axis=0
    )
    two = jnp.concatenate(
        [total[(2 * c + 1) * chunk : (2 * c + 2) * chunk, :] for c in range(chunks)], axis=0
    )
    scale = half ** (-0.5)
    one = jnp.where(low, one, swap(one)) * scale
    two = jnp.where(low, two, swap(two)) * scale
    spread = spread_slots(one, two, first, second, normed.shape[1] // lanes).astype(bf16)
    grad_wq[...] = tn(normed[...], spread).astype(bf16)
    grad_n[...] = nt(spread, wq[...]) + nn(dlog[...], wroute[...])


def spread_slots(one, two, first, second, pairs):
    upper = (lane_ids(one.shape[0]) >= half).astype(jnp.int32)
    out = []
    for g in range(pairs):
        expert = 2 * g + upper
        out.append(jnp.where(first == expert, one, jnp.where(second == expert, two, 0.0)))
    return jnp.concatenate(out, axis=1)


def key_back_kernel(piece_count, own, *rest):
    q_parts = rest[:piece_count]
    do_parts = rest[piece_count : 2 * piece_count]
    grad_kv, keys, values, total_k, total_v, seg = rest[2 * piece_count :]
    rows = own.shape[0] - pad_rows
    chunks = rows // chunk
    across = rows // lanes
    kv = own[0:rows, :]
    low = lane_ids(rows) < half
    other = swap(kv.astype(f32)).astype(bf16)
    zero = jnp.zeros_like(kv)
    pairs = ((jnp.where(low, kv, zero), jnp.where(low, zero, other)), (jnp.where(low, other, zero), jnp.where(low, zero, kv)))
    for ref, (one, two) in ((keys, pairs[0]), (values, pairs[1])):
        for c in range(chunks):
            ref[2 * c * chunk : (2 * c + 1) * chunk, :] = one[c * chunk : (c + 1) * chunk]
            ref[(2 * c + 1) * chunk : (2 * c + 2) * chunk, :] = two[c * chunk : (c + 1) * chunk]
    total_k[...] = jnp.zeros(total_k.shape, f32)
    total_v[...] = jnp.zeros(total_v.shape, f32)
    seg[...] = column(id_row(own, rows))

    def visit(index, i, message, uniform):
        queries = message[0:rows, :]
        sent = do_parts[index].at[i]
        grads = sent[0:rows, :]
        stats = sent[rows : rows + stat_rows, :].astype(f32)

        def stat(first, terms):
            block = stats[first * 8 : first * 8 + 8]
            for t in range(1, terms):
                block = block + stats[(first + t) * 8 : (first + t) * 8 + 8]
            return from_rows(block, across)

        lse = (stat(0, 3), stat(3, 3))
        delta = (stat(6, 2), stat(8, 2))
        if not uniform:
            query_ids = id_row(message, rows)

        def spread(pair):
            return jnp.concatenate(
                [jnp.broadcast_to(pair[0], (chunk, rows)), jnp.broadcast_to(pair[1], (chunk, rows))],
                axis=0,
            )

        @pl.loop(0, chunks)
        def _(c):
            at = pl.ds(pl.multiple_of(c * 2 * chunk, 2 * chunk), 2 * chunk)
            scores = nt(keys[at, :], queries) - spread(lse)
            if not uniform:
                mine = seg[pl.ds(pl.multiple_of(c * chunk, chunk), chunk), :]
                allowed = wide(jnp.concatenate([mine, mine], axis=0), across) == query_ids
                scores = jnp.where(allowed, scores, masked)
            prob = jnp.exp(scores)
            grad_prob = nt(values[at, :], grads) - spread(delta)
            total_v[at, :] += nn(prob.astype(bf16), grads)
            total_k[at, :] += nn((prob * grad_prob).astype(bf16), queries)

    over_pieces(q_parts, rows, own, visit)
    low = lane_ids(chunk) < half
    for c in range(chunks):
        one = slice(2 * c * chunk, (2 * c + 1) * chunk)
        two = slice((2 * c + 1) * chunk, (2 * c + 2) * chunk)
        key_one, key_two = total_k[one, :], total_k[two, :]
        value_one, value_two = total_v[one, :], total_v[two, :]
        grad_kv[c * chunk : (c + 1) * chunk, :] = jnp.where(
            low, key_one + swap(key_two), swap(value_one) + value_two
        ).astype(bf16)


def middle_kernel(
    tok, cot, heads, gates, picks, lse, normed, wout, wup, bup, wdown, bdown, gain, shift,
    layer_out, grad_up, grad_down, grad_out, grad_mid, dom, delta_out, dlog, grad_route,
    grad_bup, grad_small,
    second_n, second_t, total_y, total_n, mid_keep, mixed_keep,
):
    rows = tok.shape[0]
    width = tok.shape[1]
    lane = lane_ids(rows)
    low = lane < half
    first = picks[0]
    second = picks[1]
    gated = gates[...] * heads[...]
    turned = swap(gated)
    pairs = width // lanes
    mixed = spread_slots(
        jnp.where(low, gated, turned), jnp.where(low, turned, gated), first, second, pairs
    ).astype(bf16)
    mixed_keep[...] = mixed
    middle = tok[...].astype(f32) + nn(mixed, wout[...])
    mid_keep[...] = middle
    unit, _ = normalized(middle)
    n_two = (unit * gain[...] + shift[...]).astype(bf16)
    second_n[...] = n_two
    second_t[...] = n_two.T
    total_y[...] = jnp.zeros(total_y.shape, f32)
    total_n[...] = jnp.zeros(total_n.shape, f32)
    step = 256
    hidden = wup.shape[1]
    root = 0.7978845608028654
    cubic = 0.044715

    @pl.loop(0, hidden // step)
    def _(f):
        at = pl.ds(pl.multiple_of(f * step, step), step)
        up = wup[:, at]
        down = wdown[at, :]
        dy = cot[...]
        pre = nn(second_n[...], up) + bup[:, at]
        square = pre * pre
        bent = jnp.tanh(root * (pre + cubic * (square * pre)))
        act = (0.5 * pre * (1.0 + bent)).astype(bf16)
        slope = 0.5 * (1.0 + bent) + (0.5 * root) * pre * (1.0 - bent * bent) * (
            1.0 + (3.0 * cubic) * square
        )
        total_y[...] += nn(act, down)
        grad_down[at, :] = tn(act, dy).astype(bf16)
        grad_pre = (nt(dy, down) * slope).astype(bf16)
        grad_bup[:, at] = jnp.sum(grad_pre.astype(f32), axis=0, keepdims=True)
        grad_up[:, at] = nn(second_t[...], grad_pre).astype(bf16)
        total_n[...] += nt(grad_pre, up)

    middle = mid_keep[...]
    layer_out[...] = (middle + total_y[...] + bdown[...]).astype(bf16)
    unit, inverse = normalized(middle)
    back, grad_gain, grad_shift = normalized_back(total_n[...], unit, inverse, gain[...])
    dy = cot[...].astype(f32)
    grad_middle = dy + back
    grad_mid[...] = grad_middle
    grad_small[0:1, :] = jnp.sum(dy, axis=0, keepdims=True)
    grad_small[1:2, :] = grad_gain
    grad_small[2:3, :] = grad_shift
    grad_small[3:8, :] = jnp.zeros((5, width), f32)
    grad_low = grad_middle.astype(bf16)
    grad_out[...] = tn(mixed_keep[...], grad_low).astype(bf16)
    grad_mixed = nt(grad_low, wout[...])
    one = jnp.zeros((rows, lanes), f32)
    two = jnp.zeros((rows, lanes), f32)
    for g in range(pairs):
        part = grad_mixed[:, g * lanes : (g + 1) * lanes]
        one = jnp.where(first // 2 == g, part, one)
        two = jnp.where(second // 2 == g, part, two)
    one = jnp.where(first % 2 == 0, one, swap(one))
    two = jnp.where(second % 2 == 1, two, swap(two))
    slots = jnp.where(low, one, two)
    head_values = heads[...]
    gate = gates[...]
    grad_heads = (gate * slots).astype(bf16)
    dom[0:rows, :] = grad_heads
    gated_grad = slots * head_values
    gate_one = jnp.sum(jnp.where(low, gated_grad, 0.0), axis=1, keepdims=True)
    gate_two = jnp.sum(jnp.where(low, 0.0, gated_grad), axis=1, keepdims=True)
    grad_gate = jnp.where(low, gate_one, gate_two)
    weighted = gate * grad_gate
    mean_grad = weighted + swap(weighted)
    grad_logit = gate * (grad_gate - mean_grad)
    logit_other = swap(grad_logit)
    logit_one = jnp.where(low, grad_logit, logit_other)
    logit_two = jnp.where(low, logit_other, grad_logit)
    grad_logits = jnp.where(
        lane == first, logit_one, jnp.where(lane == second, logit_two, 0.0)
    ).astype(bf16)
    experts = dlog.shape[1]
    dlog[...] = grad_logits[:, :experts]
    grad_route[...] = tn(grad_logits, normed[...])[:experts, :]
    carried = grad_heads.astype(f32) * head_values
    deltas = (
        jnp.sum(jnp.where(low, carried, 0.0), axis=1, keepdims=True),
        jnp.sum(jnp.where(low, 0.0, carried), axis=1, keepdims=True),
    )
    terms = []
    for j in range(2):
        wide_delta = jnp.broadcast_to(deltas[j], (rows, lanes))
        parts = []
        for c in range(rows // chunk):
            at = slice((2 * c + j) * chunk, (2 * c + j + 1) * chunk)
            delta_out[at, :] = wide_delta[c * chunk : (c + 1) * chunk]
            parts.append(lse[at, :])
        terms.append((split(row_of(jnp.concatenate(parts, axis=0)), 3), split(row_of(wide_delta), 2)))
    blocks = terms[0][0] + terms[1][0] + terms[0][1] + terms[1][1]
    dom[rows : rows + stat_rows, :] = jnp.concatenate(
        [to_rows(b) for b in blocks], axis=0
    ).astype(bf16)


def row_of(replicated):
    return jnp.transpose(replicated, (1, 0))[0:1, :]


def split(row, terms):
    out = []
    for _ in range(terms):
        part = row.astype(bf16).astype(f32)
        out.append(part)
        row = row - part
    return out


def final_kernel(tok, normed, grad_n, grad_kv, grad_mid, wkv, gain, grad_tokens, grad_wkv, small):
    width = tok.shape[1]
    low = grad_kv[...]
    grad_wkv[...] = tn(normed[...], low)
    upstream = grad_n[...] + nt(low, wkv[...])
    unit, inverse = normalized(tok[...].astype(f32))
    back, grad_gain, grad_shift = normalized_back(upstream, unit, inverse, gain[...])
    grad_tokens[...] = grad_mid[...] + back
    small[0:1, :] = grad_gain
    small[1:2, :] = grad_shift
    small[2:8, :] = jnp.zeros((6, width), f32)


def call(kernel, out_shape, scratch, limit, flops, *operands):
    moved = sum(x.size * x.dtype.itemsize for x in operands)
    whole = pl.BlockSpec(memory_space=pltpu.VMEM)
    return pl.pallas_call(
        kernel,
        out_shape=out_shape,
        in_specs=[whole] * len(operands),
        out_specs=jax.tree.map(lambda _: whole, out_shape),
        scratch_shapes=scratch,
        compiler_params=pltpu.CompilerParams(vmem_limit_bytes=limit),
        cost_estimate=pl.CostEstimate(flops=flops, bytes_accessed=moved, transcendentals=0),
    )(*operands)


def shape(dims, dtype):
    return jax.ShapeDtypeStruct(tuple(dims), dtype)


def gather(message, size):
    if size > 16:
        return [lax.all_gather(message, "seq", axis=0, tiled=False)]
    parts = [message[None]]
    for offset in range(1, size):
        if size & (size - 1) == 0:
            pairs = [(i, i ^ offset) for i in range(size)]
        else:
            pairs = [(i, (i + offset) % size) for i in range(size)]
        parts.append(lax.ppermute(message, "seq", pairs)[None])
    return parts


def local(
    tokens, cotangent, w_query, w_kv, w_route, w_out, w_up, bias_up, w_down, bias_down,
    gain_one, shift_one, gain_two, shift_two, choices, segment_ids,
):
    size = lax.axis_size("seq")
    tok, cot = tokens[0], cotangent[0]
    rows, width = tok.shape
    hidden = w_up.shape[1]
    route = w_route.T
    experts = route.shape[0]
    row = lambda v: v.reshape(1, -1)
    message = shape((rows + pad_rows, lanes), bf16)
    kvm, qm, normed, gates, picks = call(
        project_kernel,
        (message, message, shape((rows, width), bf16), shape((rows, lanes), f32), shape((2, rows, lanes), jnp.int32)),
        [], 32 * mib, 2 * rows * width * (width + lanes),
        tok, w_query, w_kv, route, row(gain_one), row(shift_one), choices[0].T, segment_ids,
    )
    kv_parts = gather(kvm, size)
    q_parts = gather(qm, size)
    count = len(kv_parts)
    stacked = (2 * rows, lanes)
    attention_flops = 2 * 2 * rows * rows * size * lanes
    heads, lse = call(
        functools.partial(forward_kernel, count),
        (shape((rows, lanes), f32), shape(stacked, f32)),
        [pltpu.VMEM(stacked, bf16), pltpu.VMEM(stacked, f32), pltpu.VMEM(stacked, f32), pltpu.VMEM((rows, lanes), f32)],
        40 * mib, 2 * attention_flops,
        qm, kvm, *kv_parts,
    )
    (
        layer_out, grad_up, grad_down, grad_out, grad_mid, dom, delta, dlog, grad_route, grad_bup, small_two,
    ) = call(
        middle_kernel,
        (
            shape((rows, width), bf16), shape((width, hidden), bf16), shape((hidden, width), bf16),
            shape((width, width), bf16), shape((rows, width), f32), shape((rows + stat_rows, lanes), bf16),
            shape(stacked, f32), shape((rows, experts), bf16), shape((experts, width), f32),
            shape((1, hidden), f32), shape((8, width), f32),
        ),
        [
            pltpu.VMEM((rows, width), bf16), pltpu.VMEM((width, rows), bf16), pltpu.VMEM((rows, width), f32),
            pltpu.VMEM((rows, width), f32), pltpu.VMEM((rows, width), f32), pltpu.VMEM((rows, width), bf16),
        ],
        56 * mib, 12 * rows * width * hidden,
        tok, cot, heads, gates, picks, lse, normed, w_out, w_up, row(bias_up), w_down, row(bias_down),
        row(gain_two), row(shift_two),
    )
    grad_up, grad_down, grad_out = lax.psum((grad_up, grad_down, grad_out), ("seq", "row"))
    do_parts = gather(dom, size)
    grad_wq, grad_n = call(
        functools.partial(query_back_kernel, count),
        (shape((width, width), bf16), shape((rows, width), f32)),
        [pltpu.VMEM(stacked, bf16), pltpu.VMEM(stacked, bf16), pltpu.VMEM(stacked, f32), pltpu.VMEM((rows, lanes), f32)],
        40 * mib, 3 * attention_flops,
        qm, dom, lse, delta, normed, picks, w_query, dlog, route, kvm, *kv_parts,
    )
    grad_kv = call(
        functools.partial(key_back_kernel, count),
        shape((rows, lanes), bf16),
        [
            pltpu.VMEM(stacked, bf16), pltpu.VMEM(stacked, bf16), pltpu.VMEM(stacked, f32),
            pltpu.VMEM(stacked, f32), pltpu.VMEM((rows, lanes), f32),
        ],
        56 * mib, 4 * attention_flops,
        kvm, *q_parts, *do_parts,
    )
    grad_tokens, grad_wkv, small_one = call(
        final_kernel,
        (shape((rows, width), f32), shape((width, lanes), f32), shape((8, width), f32)),
        [], 32 * mib, 4 * rows * width * lanes,
        tok, normed, grad_n, grad_kv, grad_mid, w_kv, row(gain_one),
    )
    grad_wq, grad_wkv, grad_route, grad_bup, small_two, small_one = lax.psum(
        (grad_wq.astype(f32), grad_wkv, grad_route, grad_bup, small_two, small_one), ("seq", "row")
    )
    return (
        layer_out[None],
        grad_tokens[None],
        grad_wq,
        grad_wkv,
        grad_route.T,
        grad_out.astype(f32),
        grad_up.astype(f32),
        grad_bup.reshape(-1),
        grad_down.astype(f32),
        small_two[0],
        small_one[0],
        small_one[1],
        small_two[1],
        small_two[2],
    )


def solution(mesh):
    split_tokens = P("row", "seq", None)
    placed = (split_tokens, split_tokens) + (P(),) * 12 + (split_tokens, P("row", "seq"))
    return jax.shard_map(
        local,
        mesh=mesh,
        in_specs=placed,
        out_specs=(split_tokens, split_tokens) + (P(),) * 12,
        check_vma=False,
    )
```

time: 681 us -> 441 us (0.65)
  matrix products: 199 us -> 0 us
  local copies, waits for them, and re-layouts: 105 us -> 18.7 us
  starting transfers between devices: 0.12 us -> 55.6 us
  Pallas kernels: 0 us -> 54.1 us
  other arithmetic: 53.2 us -> 7.99 us
  loops' own time: 16.4 us -> 0 us
  blocking collectives: 73.2 us -> 85.6 us
  waiting for transfers between devices: 208 us -> 196 us
    dot_general x80 -> x0, matrix products: 199 us -> none  [the longest x8 29.2 us: backward_terms(): jnp.einsum('jtd,kd->jtk', grad_heads, key_part[:, head_size:], preferred_...]
    ppermute x0 -> x21, waiting for transfers between devices: none -> 62 us  [gather(): parts.append(lax.ppermute(message, 'seq', pairs)[None])]
    ppermute x0 -> x21, starting transfers between devices: none -> 55.5 us  [gather(): parts.append(lax.ppermute(message, 'seq', pairs)[None])]
    pallas_call x0 -> x6, Pallas kernels: none -> 54.1 us  [call(): pl.pallas_call(kernel, out_shape=out_shape, in_specs=[whole] * len(operan...]
    reduce_scatter x1 -> x0, waiting for transfers between devices: 49 us -> none  [local(): key_grads = lax.psum_scatter(buffer, 'seq', scatter_dimension=0, tiled=True)]
    psum x1, blocking collectives: 41.1 us -> 85.6 us  [local(): lax.psum((grad_wq.astype(f32), grad_wkv, grad_route, grad_bup, small_two,...]
    all_gather x1 -> x0, blocking collectives: 32.1 us -> none  [local(): lax.all_gather(seg_query, 'seq', axis=0, tiled=True)]
    reduce_sum x15 -> x0, other arithmetic: 31.1 us -> none  [the longest x8 23.5 us: update(): totals = totals * factor + jnp.sum(weights, axis=-1)]
  transfers between devices with their start and end apart: 3 -> 23, of which waited for: 2 -> 12; matrix products, arithmetic and copies ran while one was open for 10% -> 2% of each run, Pallas kernels for 0% -> 5%
where the time goes in v1:
time: 441 us; the launch traced here: 433 us
  waiting for transfers between devices  196 us (44%)
  blocking collectives  85.6 us (19%)
  starting transfers between devices  55.6 us (13%)
  Pallas kernels  54.1 us (12%)
  local copies, waits for them, and re-layouts  18.7 us (4%)
  between operations  14.8 us (3%)
  other arithmetic  7.99 us (2%)
    psum x1, waiting for transfers between devices, local(): lax.psum((grad_wq.astype(f32), grad_wkv, grad_route, grad_bup, small_two,...  122 us
    psum x1, blocking collectives, local(): lax.psum((grad_wq.astype(f32), grad_wkv, grad_route, grad_bup, small_two,...  85.6 us
    ppermute x21, waiting for transfers between devices, gather(): parts.append(lax.ppermute(message, 'seq', pairs)[None])  62 us
    ppermute x21, starting transfers between devices, gather(): parts.append(lax.ppermute(message, 'seq', pairs)[None])  55.5 us
    pallas_call x6, Pallas kernels, call(): pl.pallas_call(kernel, out_shape=out_shape, in_specs=[whole] * len(operan...  54.1 us
    unnamed x95, local copies, waits for them, and re-layouts  18.1 us
    psum x1, waiting for transfers between devices, local(): lax.psum((grad_up, grad_down, grad_out), ('seq', 'row'))  12 us
  transfers between devices with their start and end apart: 23, of which 12 were waited for; matrix products, arithmetic and copies ran while one was open for 2% of the time, Pallas kernels for 5%

profile of v1, /device:TPU:0, one launch (start us, length us, event | category | flops | bytes accessed | tf_op | source)
XLA Modules:
  0.0 433.3 jit_solution(7482586316741067080)
XLA Ops:
  18.3 4.0 collective-permute-start.2
  22.3 2.6 collective-permute-start.3
  25.1 2.5 collective-permute-start.5
  31.7 13.1 %collective-permute-done.3 = bf16[656,128]{1,0:T(8,128)(2,1)S(1)} collective-permute-done((bf16[656,128]{1,0:T(8,128)(2,1)S(1)}, bf16[656,128]{1,0:T(8,128)(2,1)S(1)}, u32[]{:S(2)}, u32[]{:S(2)}) %collective-permute-start.3) | collective-permute-done | bytes 167968 | tf_op jit(solution)/shard_map/ppermute | solution.py:509
  44.8 2.9 collective-permute-done.4
  50.1 7.5 %shard_map.264 = (f32[640,128]{1,0:T(8,128)S(1)}, f32[1280,128]{1,0:T(8,128)S(1)}) custom-call(bf16[656,128]{1,0:T(8,128)(2,1)S(1)} %get-tuple-element.37.qm, bf16[656,128]{1,0:T(8,128)(2,1)S(1)} %get-tuple-element.38.own, bf16[1,656,128]{2,1,0:T(8,128)(2,1)S(1)} %bitcast.51, bf16[1,656,128]{2,1,0:T(8,128)(2,1)S(1)} %bitcast.64, ...), custom_call_target="tpu_custom_call" | custom-call | flops 3355443200 | bytes 1679360 | tf_op jit(solution)/shard_map/pallas_call | solution.py:485
  59.2 24.5 %shard_map.265 = (bf16[640,512]{1,0:T(8,128)(2,1)}, bf16[512,2048]{1,0:T(8,128)(2,1)}, bf16[2048,512]{1,0:T(8,128)(2,1)}, bf16[512,512]{1,0:T(8,128)(2,1)}, f32[...) custom-call(bf16[640,512]{1,0:T(8,128)(2,1)} %bitcast.45, ...), custom_call_target="tpu_custom_call" | custom-call | flops 8053063680 | bytes 8665088 | tf_op jit(solution)/shard_map/pallas_call | solution.py:485
  83.9 2.7 collective-permute-start.7
  86.6 16.6 %collective-permute-start.8 = (bf16[656,128]{1,0:T(8,128)(2,1)S(1)}, bf16[656,128]{1,0:T(8,128)(2,1)S(1)}, u32[]{:S(2)}, u32[]{:S(2)}) collective-permute-start(bf16[656,128]{1,0:T(8,128)(2,1)S(1)} %get-tuple-element.37.qm), channel_id=1, source_target_pairs={{0,8},{4,12},{8,0},{12,4},{16,24},{20,28},{24,16},{28,20},{1,9},{5... | collective-permute-start | bytes 503816 | tf_op jit(solution)/shard_map/ppermute | solution.py:509
  105.8 2.8 collective-permute-start.15
  111.0 11.9 %collective-permute-done.9 = bf16[656,128]{1,0:T(8,128)(2,1)S(1)} collective-permute-done((bf16[656,128]{1,0:T(8,128)(2,1)S(1)}, bf16[656,128]{1,0:T(8,128)(2,1)S(1)}, u32[]{:S(2)}, u32[]{:S(2)}) %collective-permute-start.9) | collective-permute-done | bytes 167968 | tf_op jit(solution)/shard_map/ppermute | solution.py:509
  122.9 10.3 %collective-permute-done.11 = bf16[656,128]{1,0:T(8,128)(2,1)S(1)} collective-permute-done((bf16[656,128]{1,0:T(8,128)(2,1)S(1)}, bf16[656,128]{1,0:T(8,128)(2,1)S(1)}, u32[]{:S(2)}, u32[]{:S(2)}) %collective-permute-start.11) | collective-permute-done | bytes 167968 | tf_op jit(solution)/shard_map/ppermute | solution.py:509
  133.6 6.2 %collective-permute-done.12 = bf16[656,128]{1,0:T(8,128)(2,1)S(1)} collective-permute-done((bf16[656,128]{1,0:T(8,128)(2,1)S(1)}, bf16[656,128]{1,0:T(8,128)(2,1)S(1)}, u32[]{:S(2)}, u32[]{:S(2)}) %collective-permute-start.12) | collective-permute-done | bytes 167968 | tf_op jit(solution)/shard_map/ppermute | solution.py:509
  142.2 2.6 collective-permute-done.13
  144.8 11.1 %collective-permute-start.18 = (bf16[720,128]{1,0:T(8,128)(2,1)S(1)}, bf16[720,128]{1,0:T(8,128)(2,1)S(1)}, u32[]{:S(2)}, u32[]{:S(2)}) collective-permute-start(bf16[720,128]{1,0:T(8,128)(2,1)S(1)} %copy-done.12), channel_id=1, source_target_pairs={{0,20},{4,16},{8,28},{12,24},{16,4},{20,0},{24,12},{28,8},{1,21},{... | collective-permute-start | bytes 552968 | tf_op jit(solution)/shard_map/ppermute | solution.py:509
  161.5 7.9 %shard_map.266 = (bf16[512,512]{1,0:T(8,128)(2,1)S(1)}, f32[640,512]{1,0:T(8,128)S(1)}) custom-call(bf16[656,128]{1,0:T(8,128)(2,1)S(1)} %get-tuple-element.37.qm, bf16[720,128]{1,0:T(8,128)(2,1)S(1)} %copy-done.12, f32[1280,128]{1,0:T(8,128)S(1)} %copy-done.24, f32[1280,128]{1,0:T(8,128)S(1)} %copy-done.25, bf16[640,512]{1,0:T(8,128)(2,1)S(1)} %copy-done.4, ...), custom_call_target="tpu_custom_call" | custom-call | flops 5033164800 | bytes 5027840 | tf_op jit(solution)/shard_map/pallas_call | solution.py:485
  169.5 5.5 %collective-permute-done.17 = bf16[720,128]{1,0:T(8,128)(2,1)S(1)} collective-permute-done((bf16[720,128]{1,0:T(8,128)(2,1)S(1)}, bf16[720,128]{1,0:T(8,128)(2,1)S(1)}, u32[]{:S(2)}, u32[]{:S(2)}) %collective-permute-start.17) | collective-permute-done | bytes 184352 | tf_op jit(solution)/shard_map/ppermute | solution.py:509
  175.0 6.9 %collective-permute-done.18 = bf16[720,128]{1,0:T(8,128)(2,1)S(1)} collective-permute-done((bf16[720,128]{1,0:T(8,128)(2,1)S(1)}, bf16[720,128]{1,0:T(8,128)(2,1)S(1)}, u32[]{:S(2)}, u32[]{:S(2)}) %collective-permute-start.18) | collective-permute-done | bytes 184352 | tf_op jit(solution)/shard_map/ppermute | solution.py:509
  182.7 9.8 %shard_map.267.grad_kv = bf16[640,128]{1,0:T(8,128)(2,1)} custom-call(bf16[656,128]{1,0:T(8,128)(2,1)} %copy-done.13, bf16[1,656,128]{2,1,0:T(8,128)(2,1)} %bitcast.53, bf16[1,656,128]{2,1,0:T(8,128)(2,1)} %bitcast.88, bf16[1,656,128]{2,1,0:T(8,128)(2,1)} %bitcast.89, bf16[1,656,128]{2,1,0:T(8,128)(2,1)} %bitcast.90, bf16[1,656,128]{2,1,0:T(8,128)(2,1)} %bitcast.91, ...), custom_call_target="tpu_custom_call" | custom-call | flops 6710886400 | bytes 2985984 | tf_op jit(solution)/shard_map/pallas_call | solution.py:485
  195.8 85.6 %all-reduce.9 = (f32[512,512]{1,0:T(8,128)}, f32[512,8]{0,1:T(8,128)}, f32[2048]{0:T(1024)}, f32[8,512]{1,0:T(8,128)S(1)}, f32[8,512]{1,0:T(8,128)S(1)}) all-reduce(bf16[512,512]{1,0:T(8,128)(2,1)S(1)} %get-tuple-element.51, f32[512,8]{0,1:T(8,128)S(1)} %bitcast.72, ...), channel_id=1, replica_groups=mesh['seq'=8,'row'=4] {'seq','row'}, use_global_device_ids=true, to_apply=%region_0.0 | all-reduce | flops 276480 | bytes 1687552 | tf_op jit(solution)/shard_map/psum | solution.py:586
  282.0 12.0 %all-reduce.8.cloned.1.call-done = (bf16[512,512]{1,0:T(8,128)(2,1)}, bf16[512,2048]{1,0:T(8,128)(2,1)}, bf16[2048,512]{1,0:T(8,128)(2,1)}) async-done(((bf16[512,512]{1,0:T(8,128)(2,1)}, bf16[512,2048]{1,0:T(8,128)(2,1)}, bf16[2048,512]{1,0:T(8,128)(2,1)}), (bf16[512,512]{1,0:T(8,128)(2,1)}, bf16[512,2048]{1,0:T(8,128)(2,1)}, bf16[2048,512]{1,0:T(8,128)(2,1)})) %all-reduce.8.cloned.1.call-update) | async-done | bytes 4718608 | tf_op jit(solution)/shard_map/psum | solution.py:561
  294.0 4.3 convert_element_type.14
  298.3 2.6 convert_element_type.15
  302.0 122.4 %all-reduce.6.cloned.1.call-done = f32[512,128]{1,0:T(8,128)} async-done(((f32[512,128]{1,0:T(8,128)}), f32[512,128]{1,0:T(8,128)}) %all-reduce.6.cloned.1.call-update) | async-done | bytes 262160 | tf_op jit(solution)/shard_map/psum | solution.py:586
  (130 shorter events, 40.2 us)
Async XLA Ops:
  7.2 286.8 %all-reduce.8.cloned.1.call-start = ((), (), s32[]{:S(2)}) async-start(), calls=%async_computation.1 | async-start | bytes 9437184 | tf_op jit(solution)/shard_map/psum | solution.py:561
  18.3 139.0 %copy-start.14 = (bf16[656,128]{1,0:T(8,128)(2,1)}, bf16[656,128]{1,0:T(8,128)(2,1)S(1)}, u32[]{:S(2)}) copy-start(bf16[656,128]{1,0:T(8,128)(2,1)S(1)} %get-tuple-element.37.qm) | copy-start | bytes 503812
  18.3 11.7 %collective-permute-start.2 = (bf16[656,128]{1,0:T(8,128)(2,1)S(1)}, bf16[656,128]{1,0:T(8,128)(2,1)S(1)}, u32[]{:S(2)}, u32[]{:S(2)}) collective-permute-start(bf16[656,128]{1,0:T(8,128)(2,1)S(1)} %get-tuple-element.38.own), channel_id=1, source_target_pairs={{0,12},{4,8},{8,4},{12,0},{16,28},{20,24},{24,20},{28,16},{1,13},{... | collective-permute-start | bytes 503816 | tf_op jit(solution)/shard_map/ppermute | solution.py:509
  22.3 22.5 %collective-permute-start.3 = (bf16[656,128]{1,0:T(8,128)(2,1)S(1)}, bf16[656,128]{1,0:T(8,128)(2,1)S(1)}, u32[]{:S(2)}, u32[]{:S(2)}) collective-permute-start(bf16[656,128]{1,0:T(8,128)(2,1)S(1)} %get-tuple-element.38.own), channel_id=1, source_target_pairs={{0,16},{4,20},{8,24},{12,28},{16,0},{20,4},{24,8},{28,12},{1,17},{... | collective-permute-start | bytes 503816 | tf_op jit(solution)/shard_map/ppermute | solution.py:509
  24.9 22.8 %collective-permute-start.4 = (bf16[656,128]{1,0:T(8,128)(2,1)S(1)}, bf16[656,128]{1,0:T(8,128)(2,1)S(1)}, u32[]{:S(2)}, u32[]{:S(2)}) collective-permute-start(bf16[656,128]{1,0:T(8,128)(2,1)S(1)} %get-tuple-element.38.own), channel_id=1, source_target_pairs={{0,20},{4,16},{8,28},{12,24},{16,4},{20,0},{24,12},{28,8},{1,21},{... | collective-permute-start | bytes 503816 | tf_op jit(solution)/shard_map/ppermute | solution.py:509
  25.1 22.6 %collective-permute-start.5 = (bf16[656,128]{1,0:T(8,128)(2,1)S(1)}, bf16[656,128]{1,0:T(8,128)(2,1)S(1)}, u32[]{:S(2)}, u32[]{:S(2)}) collective-permute-start(bf16[656,128]{1,0:T(8,128)(2,1)S(1)} %get-tuple-element.38.own), channel_id=1, source_target_pairs={{0,24},{4,28},{8,16},{12,20},{16,8},{20,12},{24,0},{28,4},{1,25},{... | collective-permute-start | bytes 503816 | tf_op jit(solution)/shard_map/ppermute | solution.py:509
  27.6 20.1 %collective-permute-start.6 = (bf16[656,128]{1,0:T(8,128)(2,1)S(1)}, bf16[656,128]{1,0:T(8,128)(2,1)S(1)}, u32[]{:S(2)}, u32[]{:S(2)}) collective-permute-start(bf16[656,128]{1,0:T(8,128)(2,1)S(1)} %get-tuple-element.38.own), channel_id=1, source_target_pairs={{0,28},{4,24},{8,20},{12,16},{16,12},{20,8},{24,4},{28,0},{1,29},{... | collective-permute-start | bytes 503816 | tf_op jit(solution)/shard_map/ppermute | solution.py:509
  30.0 17.7 %collective-permute-start = (bf16[656,128]{1,0:T(8,128)(2,1)S(1)}, bf16[656,128]{1,0:T(8,128)(2,1)S(1)}, u32[]{:S(2)}, u32[]{:S(2)}) collective-permute-start(bf16[656,128]{1,0:T(8,128)(2,1)S(1)} %get-tuple-element.38.own), channel_id=1, source_target_pairs={{0,4},{4,0},{8,12},{12,8},{16,20},{20,16},{24,28},{28,24},{1,5},{5... | collective-permute-start | bytes 503816 | tf_op jit(solution)/shard_map/ppermute | solution.py:509
  44.8 5.4 %collective-permute-start.1 = (bf16[656,128]{1,0:T(8,128)(2,1)S(1)}, bf16[656,128]{1,0:T(8,128)(2,1)S(1)}, u32[]{:S(2)}, u32[]{:S(2)}) collective-permute-start(bf16[656,128]{1,0:T(8,128)(2,1)S(1)} %get-tuple-element.38.own), channel_id=1, source_target_pairs={{0,8},{4,12},{8,0},{12,4},{16,24},{20,28},{24,16},{28,20},{1,9},{5... | collective-permute-start | bytes 503816 | tf_op jit(solution)/shard_map/ppermute | solution.py:509
  83.8 340.6 %all-reduce.6.cloned.1.call-start = ((), (), s32[]{:S(2)}) async-start(), calls=%async_computation | async-start | bytes 524288 | tf_op jit(solution)/shard_map/psum | solution.py:586
  83.9 21.9 %collective-permute-start.7 = (bf16[656,128]{1,0:T(8,128)(2,1)S(1)}, bf16[656,128]{1,0:T(8,128)(2,1)S(1)}, u32[]{:S(2)}, u32[]{:S(2)}) collective-permute-start(bf16[656,128]{1,0:T(8,128)(2,1)S(1)} %get-tuple-element.37.qm), channel_id=1, source_target_pairs={{0,4},{4,0},{8,12},{12,8},{16,20},{20,16},{24,28},{28,24},{1,5},{5... | collective-permute-start | bytes 503816 | tf_op jit(solution)/shard_map/ppermute | solution.py:509
  86.6 22.0 %collective-permute-start.8 = (bf16[656,128]{1,0:T(8,128)(2,1)S(1)}, bf16[656,128]{1,0:T(8,128)(2,1)S(1)}, u32[]{:S(2)}, u32[]{:S(2)}) collective-permute-start(bf16[656,128]{1,0:T(8,128)(2,1)S(1)} %get-tuple-element.37.qm), channel_id=1, source_target_pairs={{0,8},{4,12},{8,0},{12,4},{16,24},{20,28},{24,16},{28,20},{1,9},{5... | collective-permute-start | bytes 503816 | tf_op jit(solution)/shard_map/ppermute | solution.py:509
  103.2 19.7 %collective-permute-start.9 = (bf16[656,128]{1,0:T(8,128)(2,1)S(1)}, bf16[656,128]{1,0:T(8,128)(2,1)S(1)}, u32[]{:S(2)}, u32[]{:S(2)}) collective-permute-start(bf16[656,128]{1,0:T(8,128)(2,1)S(1)} %get-tuple-element.37.qm), channel_id=1, source_target_pairs={{0,12},{4,8},{8,4},{12,0},{16,28},{20,24},{24,20},{28,16},{1,13},{... | collective-permute-start | bytes 503816 | tf_op jit(solution)/shard_map/ppermute | solution.py:509
  104.5 18.3 %collective-permute-start.10 = (bf16[656,128]{1,0:T(8,128)(2,1)S(1)}, bf16[656,128]{1,0:T(8,128)(2,1)S(1)}, u32[]{:S(2)}, u32[]{:S(2)}) collective-permute-start(bf16[656,128]{1,0:T(8,128)(2,1)S(1)} %get-tuple-element.37.qm), channel_id=1, source_target_pairs={{0,16},{4,20},{8,24},{12,28},{16,0},{20,4},{24,8},{28,12},{1,17},{... | collective-permute-start | bytes 503816 | tf_op jit(solution)/shard_map/ppermute | solution.py:509
  104.6 51.4 %collective-permute-start.14 = (bf16[720,128]{1,0:T(8,128)(2,1)S(1)}, bf16[720,128]{1,0:T(8,128)(2,1)S(1)}, u32[]{:S(2)}, u32[]{:S(2)}) collective-permute-start(bf16[720,128]{1,0:T(8,128)(2,1)S(1)} %copy-done.12), channel_id=1, source_target_pairs={{0,4},{4,0},{8,12},{12,8},{16,20},{20,16},{24,28},{28,24},{1,5},{5... | collective-permute-start | bytes 552968 | tf_op jit(solution)/shard_map/ppermute | solution.py:509
  105.8 50.2 %collective-permute-start.15 = (bf16[720,128]{1,0:T(8,128)(2,1)S(1)}, bf16[720,128]{1,0:T(8,128)(2,1)S(1)}, u32[]{:S(2)}, u32[]{:S(2)}) collective-permute-start(bf16[720,128]{1,0:T(8,128)(2,1)S(1)} %copy-done.12), channel_id=1, source_target_pairs={{0,8},{4,12},{8,0},{12,4},{16,24},{20,28},{24,16},{28,20},{1,9},{5... | collective-permute-start | bytes 552968 | tf_op jit(solution)/shard_map/ppermute | solution.py:509
  108.6 24.6 %collective-permute-start.11 = (bf16[656,128]{1,0:T(8,128)(2,1)S(1)}, bf16[656,128]{1,0:T(8,128)(2,1)S(1)}, u32[]{:S(2)}, u32[]{:S(2)}) collective-permute-start(bf16[656,128]{1,0:T(8,128)(2,1)S(1)} %get-tuple-element.37.qm), channel_id=1, source_target_pairs={{0,20},{4,16},{8,28},{12,24},{16,4},{20,0},{24,12},{28,8},{1,21},{... | collective-permute-start | bytes 503816 | tf_op jit(solution)/shard_map/ppermute | solution.py:509
  122.8 17.0 %collective-permute-start.12 = (bf16[656,128]{1,0:T(8,128)(2,1)S(1)}, bf16[656,128]{1,0:T(8,128)(2,1)S(1)}, u32[]{:S(2)}, u32[]{:S(2)}) collective-permute-start(bf16[656,128]{1,0:T(8,128)(2,1)S(1)} %get-tuple-element.37.qm), channel_id=1, source_target_pairs={{0,24},{4,28},{8,16},{12,20},{16,8},{20,12},{24,0},{28,4},{1,25},{... | collective-permute-start | bytes 503816 | tf_op jit(solution)/shard_map/ppermute | solution.py:509
  122.9 22.0 %collective-permute-start.13 = (bf16[656,128]{1,0:T(8,128)(2,1)S(1)}, bf16[656,128]{1,0:T(8,128)(2,1)S(1)}, u32[]{:S(2)}, u32[]{:S(2)}) collective-permute-start(bf16[656,128]{1,0:T(8,128)(2,1)S(1)} %get-tuple-element.37.qm), channel_id=1, source_target_pairs={{0,28},{4,24},{8,20},{12,16},{16,12},{20,8},{24,4},{28,0},{1,29},{... | collective-permute-start | bytes 503816 | tf_op jit(solution)/shard_map/ppermute | solution.py:509
  133.2 36.3 %collective-permute-start.16 = (bf16[720,128]{1,0:T(8,128)(2,1)S(1)}, bf16[720,128]{1,0:T(8,128)(2,1)S(1)}, u32[]{:S(2)}, u32[]{:S(2)}) collective-permute-start(bf16[720,128]{1,0:T(8,128)(2,1)S(1)} %copy-done.12), channel_id=1, source_target_pairs={{0,12},{4,8},{8,4},{12,0},{16,28},{20,24},{24,20},{28,16},{1,13},{... | collective-permute-start | bytes 552968 | tf_op jit(solution)/shard_map/ppermute | solution.py:509
  139.9 35.1 %collective-permute-start.17 = (bf16[720,128]{1,0:T(8,128)(2,1)S(1)}, bf16[720,128]{1,0:T(8,128)(2,1)S(1)}, u32[]{:S(2)}, u32[]{:S(2)}) collective-permute-start(bf16[720,128]{1,0:T(8,128)(2,1)S(1)} %copy-done.12), channel_id=1, source_target_pairs={{0,16},{4,20},{8,24},{12,28},{16,0},{20,4},{24,8},{28,12},{1,17},{... | collective-permute-start | bytes 552968 | tf_op jit(solution)/shard_map/ppermute | solution.py:509
  144.8 37.0 %collective-permute-start.18 = (bf16[720,128]{1,0:T(8,128)(2,1)S(1)}, bf16[720,128]{1,0:T(8,128)(2,1)S(1)}, u32[]{:S(2)}, u32[]{:S(2)}) collective-permute-start(bf16[720,128]{1,0:T(8,128)(2,1)S(1)} %copy-done.12), channel_id=1, source_target_pairs={{0,20},{4,16},{8,28},{12,24},{16,4},{20,0},{24,12},{28,8},{1,21},{... | collective-permute-start | bytes 552968 | tf_op jit(solution)/shard_map/ppermute | solution.py:509
  156.0 25.9 %collective-permute-start.19 = (bf16[720,128]{1,0:T(8,128)(2,1)S(1)}, bf16[720,128]{1,0:T(8,128)(2,1)S(1)}, u32[]{:S(2)}, u32[]{:S(2)}) collective-permute-start(bf16[720,128]{1,0:T(8,128)(2,1)S(1)} %copy-done.12), channel_id=1, source_target_pairs={{0,24},{4,28},{8,16},{12,20},{16,8},{20,12},{24,0},{28,4},{1,25},{... | collective-permute-start | bytes 552968 | tf_op jit(solution)/shard_map/ppermute | solution.py:509
  156.0 25.9 %collective-permute-start.20 = (bf16[720,128]{1,0:T(8,128)(2,1)S(1)}, bf16[720,128]{1,0:T(8,128)(2,1)S(1)}, u32[]{:S(2)}, u32[]{:S(2)}) collective-permute-start(bf16[720,128]{1,0:T(8,128)(2,1)S(1)} %copy-done.12), channel_id=1, source_target_pairs={{0,28},{4,24},{8,20},{12,16},{16,12},{20,8},{24,4},{28,0},{1,29},{... | collective-permute-start | bytes 552968 | tf_op jit(solution)/shard_map/ppermute | solution.py:509
  (46 other events, 805.4 us)
Sparse Core Ops, SparseCore 0:
  83.9 210.0 all-reduce.7
  301.0 123.3 all-reduce.5

commit v2 on v1

--- a/solution.py
+++ b/solution.py
@@ -168,14 +168,26 @@
             pl.loop(0, count)(one)
 
 
-def forward_kernel(piece_count, qm, own, *rest):
+def forward_kernel(piece_count, first, last, qm, own, *rest):
     parts = rest[:piece_count]
-    heads, lse, stack, peak, total, seg = rest[piece_count:]
+    rest = rest[piece_count:]
+    if not first:
+        total_in, peak_in = rest[:2]
+        rest = rest[2:]
+    if last:
+        heads, lse, total, peak, stack, seg = rest
+    else:
+        total, peak, stack, seg = rest
     rows = qm.shape[0] - pad_rows
     chunks = rows // chunk
+    across = rows // lanes
     store_stack(stack, qm[0:rows, :], 0)
-    peak[...] = jnp.full(peak.shape, lowest, f32)
-    total[...] = jnp.zeros(total.shape, f32)
+    if first:
+        peak[...] = jnp.full(peak.shape, lowest, f32)
+        total[...] = jnp.zeros(total.shape, f32)
+    else:
+        peak[...] = peak_in[...]
+        total[...] = total_in[...]
     seg[...] = column(id_row(own, rows))
 
     def visit(index, i, message, uniform):
@@ -191,15 +203,17 @@
             scores = nt(stack[at, :], kv)
             if not uniform:
                 mine = seg[pl.ds(pl.multiple_of(c * chunk, chunk), chunk), :]
-                allowed = wide(jnp.concatenate([mine, mine], axis=0), rows // lanes) == key_ids
+                allowed = wide(jnp.concatenate([mine, mine], axis=0), across) == key_ids
                 scores = jnp.where(allowed, scores, masked)
             before = peak[at, :]
             now = jnp.maximum(before, jnp.max(scores, axis=1, keepdims=True))
             peak[at, :] = now
-            weights = jnp.exp(scores - wide(now, rows // lanes)).astype(bf16)
+            weights = jnp.exp(scores - wide(now, across)).astype(bf16)
             total[at, :] = total[at, :] * jnp.exp(before - now) + nn(weights, values)
 
     over_pieces(parts, rows, own, visit)
+    if not last:
+        return
     low = lane_ids(chunk) < half
     for c in range(chunks):
         one = total[2 * c * chunk : (2 * c + 1) * chunk, :]
@@ -213,16 +227,21 @@
             lse[at, :] = peak[at, :] + jnp.log(jnp.where(low, whole, other))
 
 
-def query_back_kernel(
-    piece_count, qm, dom, lse, delta, normed, picks, wq, dlog, wroute, own, *rest
-):
+def query_back_kernel(spread_out, piece_count, first, last, qm, dom, lse, delta, own, *rest):
     parts = rest[:piece_count]
-    grad_wq, grad_n, stack, stack_do, total, seg = rest[piece_count:]
+    rest = rest[piece_count:]
+    if not first:
+        total_in = rest[0]
+        rest = rest[1:]
+    if last:
+        normed, picks, wq, dlog, wroute, keep, send, grad_n, total, stack, stack_do, seg = rest
+    else:
+        total, stack, stack_do, seg = rest
     rows = qm.shape[0] - pad_rows
     chunks = rows // chunk
     store_stack(stack, qm[0:rows, :], 0)
     store_stack(stack_do, dom[0:rows, :], 1)
-    total[...] = jnp.zeros(total.shape, f32)
+    total[...] = jnp.zeros(total.shape, f32) if first else total_in[...]
     seg[...] = column(id_row(own, rows))
     across = rows // lanes
 
@@ -244,9 +263,11 @@
             total[at, :] += nn((prob * grad_prob).astype(bf16), kv)
 
     over_pieces(parts, rows, own, visit)
+    if not last:
+        return
     low = lane_ids(rows) < half
-    first = picks[0]
-    second = picks[1]
+    first_pick = picks[0]
+    second_pick = picks[1]
     one = jnp.concatenate(
         [total[2 * c * chunk : (2 * c + 1) * chunk, :] for c in range(chunks)], axis=0
     )
@@ -256,8 +277,26 @@
     scale = half ** (-0.5)
     one = jnp.where(low, one, swap(one)) * scale
     two = jnp.where(low, two, swap(two)) * scale
-    spread = spread_slots(one, two, first, second, normed.shape[1] // lanes).astype(bf16)
-    grad_wq[...] = tn(normed[...], spread).astype(bf16)
+    spread = spread_slots(one, two, first_pick, second_pick, normed.shape[1] // lanes).astype(bf16)
+    whole = tn(normed[...], spread).astype(bf16)
+    core = place(spread_out)[0]
+    middle = whole.shape[1] // 2
+    count = whole.shape[0] // parts_of
+    for i in range(parts_of):
+        for side in range(2):
+            at = slice(((i // 2) * 2 + side) * count, ((i // 2) * 2 + side + 1) * count)
+            value = whole[i * count : (i + 1) * count, side * middle : (side + 1) * middle]
+            if spread_out:
+
+                @pl.when(core == i % 2)
+                def _(at=at, value=value):
+                    keep[at, :] = value
+
+                @pl.when(core != i % 2)
+                def _(at=at, value=value):
+                    send[at, :] = value
+            else:
+                (keep, send)[i % 2][at, :] = value
     grad_n[...] = nt(spread, wq[...]) + nn(dlog[...], wroute[...])
 
 
@@ -270,24 +309,29 @@
     return jnp.concatenate(out, axis=1)
 
 
-def key_back_kernel(piece_count, own, *rest):
+def key_back_kernel(piece_count, first, last, own, *rest):
     q_parts = rest[:piece_count]
     do_parts = rest[piece_count : 2 * piece_count]
-    grad_kv, keys, values, total_k, total_v, seg = rest[2 * piece_count :]
+    rest = rest[2 * piece_count :]
+    if not first:
+        k_in, v_in = rest[:2]
+        rest = rest[2:]
+    if last:
+        grad_kv = rest[0]
+        rest = rest[1:]
+    total_k, total_v, keys, values, seg = rest
     rows = own.shape[0] - pad_rows
     chunks = rows // chunk
     across = rows // lanes
     kv = own[0:rows, :]
-    low = lane_ids(rows) < half
-    other = swap(kv.astype(f32)).astype(bf16)
-    zero = jnp.zeros_like(kv)
-    pairs = ((jnp.where(low, kv, zero), jnp.where(low, zero, other)), (jnp.where(low, other, zero), jnp.where(low, zero, kv)))
-    for ref, (one, two) in ((keys, pairs[0]), (values, pairs[1])):
-        for c in range(chunks):
-            ref[2 * c * chunk : (2 * c + 1) * chunk, :] = one[c * chunk : (c + 1) * chunk]
-            ref[(2 * c + 1) * chunk : (2 * c + 2) * chunk, :] = two[c * chunk : (c + 1) * chunk]
-    total_k[...] = jnp.zeros(total_k.shape, f32)
-    total_v[...] = jnp.zeros(total_v.shape, f32)
+    store_stack_other(keys, kv, 0)
+    store_stack_other(values, kv, 1)
+    if first:
+        total_k[...] = jnp.zeros(total_k.shape, f32)
+        total_v[...] = jnp.zeros(total_v.shape, f32)
+    else:
+        total_k[...] = k_in[...]
+        total_v[...] = v_in[...]
     seg[...] = column(id_row(own, rows))
 
     def visit(index, i, message, uniform):
@@ -327,6 +371,8 @@
             total_k[at, :] += nn((prob * grad_prob).astype(bf16), queries)
 
     over_pieces(q_parts, rows, own, visit)
+    if not last:
+        return
     low = lane_ids(chunk) < half
     for c in range(chunks):
         one = slice(2 * c * chunk, (2 * c + 1) * chunk)
@@ -338,9 +384,21 @@
         ).astype(bf16)
 
 
+def store_stack_other(ref, kv, part):
+    rows = kv.shape[0]
+    low = lane_ids(rows) < half
+    other = swap(kv.astype(f32)).astype(bf16)
+    zero = jnp.zeros_like(kv)
+    one, two = jnp.where(low, (kv, other)[part], zero), jnp.where(low, zero, (other, kv)[part])
+    for c in range(rows // chunk):
+        ref[2 * c * chunk : (2 * c + 1) * chunk, :] = one[c * chunk : (c + 1) * chunk]
+        ref[(2 * c + 1) * chunk : (2 * c + 2) * chunk, :] = two[c * chunk : (c + 1) * chunk]
+
+
 def middle_kernel(
+    spread_out,
     tok, cot, heads, gates, picks, lse, normed, wout, wup, bup, wdown, bdown, gain, shift,
-    layer_out, grad_up, grad_down, grad_out, grad_mid, dom, delta_out, dlog, grad_route,
+    layer_out, keep, send, grad_mid, dom, delta_out, dlog, grad_route,
     grad_bup, grad_small,
     second_n, second_t, total_y, total_n, mid_keep, mixed_keep,
 ):
@@ -365,30 +423,48 @@
     second_t[...] = n_two.T
     total_y[...] = jnp.zeros(total_y.shape, f32)
     total_n[...] = jnp.zeros(total_n.shape, f32)
-    step = 256
+    step = 512
     hidden = wup.shape[1]
     root = 0.7978845608028654
     cubic = 0.044715
+    core = place(spread_out)[0]
+    down_rows = hidden // parts_of
+    up_rows = width // parts_of
+    piece = gradient_rows(width, hidden)
+
+    def put(index, at_row, at_lane, even, odd):
+        count, across = even.shape
+        target = (pl.ds(index * piece + at_row, count), slice(at_lane, at_lane + across))
+        keep[target] = jnp.where(core == 0, even, odd)
+        send[target] = jnp.where(core == 0, odd, even)
 
     @pl.loop(0, hidden // step)
     def _(f):
-        at = pl.ds(pl.multiple_of(f * step, step), step)
-        up = wup[:, at]
-        down = wdown[at, :]
-        dy = cot[...]
-        pre = nn(second_n[...], up) + bup[:, at]
-        square = pre * pre
-        bent = jnp.tanh(root * (pre + cubic * (square * pre)))
-        act = (0.5 * pre * (1.0 + bent)).astype(bf16)
-        slope = 0.5 * (1.0 + bent) + (0.5 * root) * pre * (1.0 - bent * bent) * (
-            1.0 + (3.0 * cubic) * square
-        )
-        total_y[...] += nn(act, down)
-        grad_down[at, :] = tn(act, dy).astype(bf16)
-        grad_pre = (nt(dy, down) * slope).astype(bf16)
-        grad_bup[:, at] = jnp.sum(grad_pre.astype(f32), axis=0, keepdims=True)
-        grad_up[:, at] = nn(second_t[...], grad_pre).astype(bf16)
-        total_n[...] += nt(grad_pre, up)
+        for sub in range(0, step, 256):
+            at = pl.ds(pl.multiple_of(f * step + sub, 256), 256)
+            up = wup[:, at]
+            down = wdown[at, :]
+            dy = cot[...]
+            pre = nn(second_n[...], up) + bup[:, at]
+            square = pre * pre
+            bent = jnp.tanh(root * (pre + cubic * (square * pre)))
+            act = (0.5 * pre * (1.0 + bent)).astype(bf16)
+            slope = 0.5 * (1.0 + bent) + (0.5 * root) * pre * (1.0 - bent * bent) * (
+                1.0 + (3.0 * cubic) * square
+            )
+            total_y[...] += nn(act, down)
+            grad_down = tn(act, dy).astype(bf16)
+            grad_pre = (nt(dy, down) * slope).astype(bf16)
+            grad_bup[:, at] = jnp.sum(grad_pre.astype(f32), axis=0, keepdims=True)
+            grad_up = nn(second_t[...], grad_pre).astype(bf16)
+            total_n[...] += nt(grad_pre, up)
+            for i in range(256 // (2 * down_rows)):
+                pair = grad_down[2 * i * down_rows : 2 * (i + 1) * down_rows]
+                index = f * (step // (2 * down_rows)) + sub // (2 * down_rows) + i
+                put(index, 0, 0, pair[:down_rows], pair[down_rows:])
+            for i in range(parts_of // 2):
+                pair = grad_up[2 * i * up_rows : 2 * (i + 1) * up_rows]
+                put(i, down_rows + f * up_rows, sub, pair[:up_rows], pair[up_rows:])
 
     middle = mid_keep[...]
     layer_out[...] = (middle + total_y[...] + bdown[...]).astype(bf16)
@@ -402,7 +478,10 @@
     grad_small[2:3, :] = grad_shift
     grad_small[3:8, :] = jnp.zeros((5, width), f32)
     grad_low = grad_middle.astype(bf16)
-    grad_out[...] = tn(mixed_keep[...], grad_low).astype(bf16)
+    grad_out = tn(mixed_keep[...], grad_low).astype(bf16)
+    for i in range(parts_of // 2):
+        pair = grad_out[2 * i * up_rows : 2 * (i + 1) * up_rows]
+        put(i, piece - up_rows, 0, pair[:up_rows], pair[up_rows:])
     grad_mixed = nt(grad_low, wout[...])
     one = jnp.zeros((rows, lanes), f32)
     two = jnp.zeros((rows, lanes), f32)
@@ -466,17 +545,220 @@
     return out
 
 
-def final_kernel(tok, normed, grad_n, grad_kv, grad_mid, wkv, gain, grad_tokens, grad_wkv, small):
+def final_kernel(
+    spread_out, tok, normed, grad_n, grad_kv, grad_mid, wkv, gain, grad_route, grad_bup, small_two,
+    grad_tokens, keep, send, whole,
+):
     width = tok.shape[1]
     low = grad_kv[...]
-    grad_wkv[...] = tn(normed[...], low)
+    whole[0:width, :] = tn(normed[...], low).astype(bf16)
     upstream = grad_n[...] + nt(low, wkv[...])
     unit, inverse = normalized(tok[...].astype(f32))
     back, grad_gain, grad_shift = normalized_back(upstream, unit, inverse, gain[...])
     grad_tokens[...] = grad_mid[...] + back
-    small[0:1, :] = grad_gain
-    small[1:2, :] = grad_shift
-    small[2:8, :] = jnp.zeros((6, width), f32)
+    rows = [grad_gain, grad_shift] + [small_two[i : i + 1, :] for i in range(3)]
+    rows += [grad_bup[:, i : i + width] for i in range(0, grad_bup.shape[1], width)]
+    rows += [grad_route[i : i + 1, :] for i in range(grad_route.shape[0])]
+    small = jnp.concatenate([row[:, i : i + lanes] for row in rows for i in range(0, width, lanes)], axis=0)
+    last = whole.shape[0] - width
+    small = jnp.concatenate([small, jnp.zeros((last - small.shape[0], lanes), f32)], axis=0)
+    whole[width:, :] = small.astype(bf16)
+    core = place(spread_out)[0]
+    piece = keep.shape[0]
+    keep[...] = whole[block(core, piece), :]
+    send[...] = whole[block(1 - core, piece), :]
+
+
+parts_of = 32
+
+
+def place(spread_out):
+    if not spread_out:
+        return 0, 0, 0, 0
+    row, seq = lax.axis_index("row"), lax.axis_index("seq")
+    return lax.rem(row, 2), row // 2, lax.rem(seq, 2), seq // 2
+
+
+def gradient_rows(width, hidden):
+    return hidden // parts_of + (hidden // width + 1) * (width // parts_of)
+
+
+def block(index, count):
+    return pl.ds(pl.multiple_of(index * count, 16), count)
+
+
+def plus(*refs):
+    def get(at):
+        total = refs[0][at].astype(f32)
+        for ref in refs[1:]:
+            total = total + ref[at].astype(f32)
+        return total.astype(bf16)
+
+    return get
+
+
+def after_core_kernel(keep, received, one_keep, one_send, two_keep, two_send):
+    _, x, y, _ = place(True)
+    piece = keep.shape[0] // 16
+    middle = keep.shape[1] // 2
+    left, right = slice(0, middle), slice(middle, 2 * middle)
+    total = plus(keep, received)
+    for zy in range(8):
+        here = slice(zy * piece, (zy + 1) * piece)
+        one_keep[here, :] = total((block(zy * 2 + x, piece), left))
+        one_send[here, :] = total((block(zy * 2 + 1 - x, piece), left))
+    for z in range(4):
+        for at_x in range(2):
+            here = slice((z * 2 + at_x) * piece, (z * 2 + at_x + 1) * piece)
+            two_keep[here, :] = total((block((z * 2 + y) * 2 + at_x, piece), right))
+            two_send[here, :] = total((block((z * 2 + 1 - y) * 2 + at_x, piece), right))
+
+
+def split_x_kernel(keep, received, kept, sent):
+    x = place(True)[1]
+    piece = keep.shape[0] // 16
+    total = plus(keep, received)
+    for zy in range(8):
+        here = slice(zy * piece, (zy + 1) * piece)
+        kept[here, :] = total((block(zy * 2 + x, piece), slice(None)))
+        sent[here, :] = total((block(zy * 2 + 1 - x, piece), slice(None)))
+
+
+def after_first_kernel(one, one_in, two, two_in, extra, extra_in, one_keep, one_send, two_keep, two_send):
+    _, x, y, _ = place(True)
+    for total, mine, kept, sent, piece, offset in (
+        (plus(one, one_in), y, one_keep, one_send, one.shape[0] // 8, 0),
+        (plus(extra, extra_in), y, one_keep, one_send, extra.shape[0] // 8, one.shape[0] // 8),
+        (plus(two, two_in), x, two_keep, two_send, two.shape[0] // 8, 0),
+    ):
+        stride = kept.shape[0] // 4
+        for z in range(4):
+            here = slice(z * stride + offset, z * stride + offset + piece)
+            kept[here, :] = total((block(z * 2 + mine, piece), slice(None)))
+            sent[here, :] = total((block(z * 2 + 1 - mine, piece), slice(None)))
+
+
+def after_second_kernel(one, one_in, two, two_in, *outs):
+    z = place(True)[3]
+    middle = one.shape[1]
+    piece = two.shape[0] // 4
+    stride = one.shape[0] // 4
+    more = (stride - piece) // 2
+    left, right = plus(one, one_in), plus(two, two_in)
+    for i, out in enumerate(outs):
+        base = (z ^ i) * stride
+
+        def part(offset, count):
+            return left((pl.ds(pl.multiple_of(base + offset, 16), count), slice(None)))
+
+        out[:piece, :middle] = part(0, piece)
+        out[:piece, middle:] = right((block(z ^ i, piece), slice(None)))
+        out[piece:, :middle] = part(piece, more)
+        out[piece:, middle:] = part(piece + more, more)
+
+
+def sum_kernel(*refs):
+    refs[-1][...] = plus(*refs[:-1])(Ellipsis)
+
+
+def join_halves_kernel(*refs):
+    z = place(True)[3]
+    one, two = refs[4:]
+    piece, wide_piece = refs[0].shape
+    middle = wide_piece // 2
+    for i in range(4):
+        one[block(z ^ i, piece), :] = refs[i][:, :middle]
+        two[block(z ^ i, piece), :] = refs[i][:, middle:]
+
+
+def unpack_kernel(spread_out, *refs):
+    core, x, y, _ = place(spread_out)
+    grad_up, grad_down, grad_out, grad_wq = refs[8:]
+    piece, middle = refs[0].shape[0] // 8, refs[0].shape[1]
+    width, hidden = grad_up.shape
+    down_rows, up_rows = hidden // parts_of, width // parts_of
+    for turn in range(2):
+        for outer in range(2):
+            for side in range(2):
+                ref = refs[turn * 4 + side * 2 + outer]
+                for inner in range(2):
+                    at_x, at_y = (x ^ outer, y ^ inner) if side == 0 else (x ^ inner, y ^ outer)
+                    for z in range(4):
+                        device = ((z * 2 + at_y) * 2 + at_x) * 2 + (core ^ turn)
+                        base = (inner * 4 + z) * piece
+                        lane = slice(side * middle, (side + 1) * middle)
+                        grad_down[block(device, down_rows), lane] = ref[base : base + down_rows, :].astype(f32)
+                        at = base + down_rows
+                        target = block(device, up_rows)
+                        for c in range(hidden // width):
+                            lane_up = slice(c * width + side * middle, c * width + (side + 1) * middle)
+                            grad_up[target, lane_up] = ref[at : at + up_rows, :].astype(f32)
+                            at += up_rows
+                        grad_out[target, lane] = ref[at : at + up_rows, :].astype(f32)
+                        grad_wq[target, lane] = ref[at + up_rows : at + 2 * up_rows, :].astype(f32)
+
+
+def flip_row(x, mask):
+    return lax.ppermute(x, "row", [(i, i ^ mask) for i in range(4)])
+
+
+def flip_seq(x, mask):
+    return lax.ppermute(x, "seq", [(i, i ^ mask) for i in range(8)])
+
+
+def simple(kernel, outs, *operands):
+    return call(kernel, outs, [], 48 * mib, 0, *operands)
+
+
+def add(a, b):
+    return (a.astype(f32) + b.astype(f32)).astype(bf16)
+
+
+def finish_sums(large, small):
+    mine, arrived = large
+    keep, send = small
+    count, width = mine.shape
+    total = add(keep, flip_row(send, 1))
+    total = add(total, flip_row(total, 2))
+    arrived[0] = after(arrived[0], total)
+    part = shape((4 * count, width // 2), bf16)
+    one, two = simple(join_halves_kernel, (part,) * 2, mine, *arrived)
+    one_in, two_in = flip_seq(one, 1), flip_row(two, 2)
+    total = add(total, after(flip_seq(total, 1), one))
+    one_in = after(one_in, total)
+    one, two = jnp.concatenate([one, one_in]), jnp.concatenate([two, two_in])
+    one_in, two_in = flip_row(one, 2), flip_seq(two, 1)
+    total = add(total, after(flip_seq(total, 2), one))
+    total = add(total, flip_seq(total, 4))
+    other = flip_row(total, 1)
+    one_other, two_other = flip_row(one, 1), flip_row(two, 1)
+    one_in = after(one_in, other, one_other, two_other)
+    return (
+        (one, one_in, two, two_in, one_other, flip_row(one_in, 1), two_other, flip_row(two_in, 1)),
+        (total, other),
+    )
+
+
+def unpack_small_kernel(spread_out, mine, other, grad_wkv, grad_route, grad_bup, grad_small, whole):
+    core = place(spread_out)[0]
+    piece = mine.shape[0]
+    whole[block(core, piece), :] = mine[...].astype(f32)
+    whole[block(1 - core, piece), :] = other[...].astype(f32)
+    width = grad_wkv.shape[0]
+    across = width // lanes
+    grad_wkv[...] = whole[0:width, :]
+    at = width
+    for i in range(5):
+        for g in range(across):
+            grad_small[i : i + 1, g * lanes : (g + 1) * lanes] = whole[at : at + 1, :]
+            at += 1
+    for g in range(grad_bup.shape[1] // lanes):
+        grad_bup[:, g * lanes : (g + 1) * lanes] = whole[at : at + 1, :]
+        at += 1
+    for i in range(grad_route.shape[0]):
+        for g in range(across):
+            grad_route[i : i + 1, g * lanes : (g + 1) * lanes] = whole[at : at + 1, :]
+            at += 1
 
 
 def call(kernel, out_shape, scratch, limit, flops, *operands):
@@ -497,17 +779,16 @@
     return jax.ShapeDtypeStruct(tuple(dims), dtype)
 
 
-def gather(message, size):
-    if size > 16:
-        return [lax.all_gather(message, "seq", axis=0, tiled=False)]
-    parts = [message[None]]
-    for offset in range(1, size):
-        if size & (size - 1) == 0:
-            pairs = [(i, i ^ offset) for i in range(size)]
-        else:
-            pairs = [(i, (i + offset) % size) for i in range(size)]
-        parts.append(lax.ppermute(message, "seq", pairs)[None])
-    return parts
+def after(value, *earlier):
+    return lax.optimization_barrier((value,) + earlier)[0]
+
+
+def gather_keys(kvm, size):
+    if size != 8:
+        return [[kvm[None]], [lax.all_gather(kvm, "seq", axis=0, tiled=False)]]
+    near_y, near_z, far_z = flip_seq(kvm, 1), flip_seq(kvm, 2), flip_seq(kvm, 4)
+    others = [flip_seq(near_z, 1), flip_seq(far_z, 1), flip_seq(far_z, 2), flip_seq(kvm, 7)]
+    return [[m[None] for m in (kvm, near_y, near_z, far_z)], [m[None] for m in others]]
 
 
 def local(
@@ -528,25 +809,40 @@
         [], 32 * mib, 2 * rows * width * (width + lanes),
         tok, w_query, w_kv, route, row(gain_one), row(shift_one), choices[0].T, segment_ids,
     )
-    kv_parts = gather(kvm, size)
-    q_parts = gather(qm, size)
-    count = len(kv_parts)
+    spread_out = size == 8 and lax.axis_size("row") == 4
     stacked = (2 * rows, lanes)
+    near, others = gather_keys(kvm, size)
+    all_kv = near + others
+    if size != 8:
+        near, others, all_kv = others, [], others
     attention_flops = 2 * 2 * rows * rows * size * lanes
-    heads, lse = call(
-        functools.partial(forward_kernel, count),
-        (shape((rows, lanes), f32), shape(stacked, f32)),
-        [pltpu.VMEM(stacked, bf16), pltpu.VMEM(stacked, f32), pltpu.VMEM(stacked, f32), pltpu.VMEM((rows, lanes), f32)],
-        40 * mib, 2 * attention_flops,
-        qm, kvm, *kv_parts,
-    )
+    state = (shape(stacked, f32),) * 2
+    kept = [pltpu.VMEM(stacked, bf16), pltpu.VMEM((rows, lanes), f32)]
+    finished = (shape((rows, lanes), f32), shape(stacked, f32)) + state
+    if others:
+        so_far = call(
+            functools.partial(forward_kernel, len(near), True, False), state, kept, 40 * mib, attention_flops, qm, kvm, *near
+        )
+        heads, lse, _, _ = call(
+            functools.partial(forward_kernel, len(others), False, True), finished, kept, 40 * mib, attention_flops,
+            qm, kvm, *others, *so_far,
+        )
+    else:
+        heads, lse, _, _ = call(
+            functools.partial(forward_kernel, len(near), True, True), finished, kept, 40 * mib, attention_flops, qm, kvm, *near
+        )
+    if size == 8:
+        q_two = after(jnp.stack([qm, flip_seq(qm, 1)]), so_far[0])
+        q_far = [flip_seq(q_two, 2), flip_seq(q_two, 4)]
+        heads = after(heads, q_two)
+    piece = gradient_rows(width, hidden)
+    gradients = shape((piece * parts_of // 2, width), bf16)
     (
-        layer_out, grad_up, grad_down, grad_out, grad_mid, dom, delta, dlog, grad_route, grad_bup, small_two,
+        layer_out, keep, send, grad_mid, dom, delta, dlog, grad_route, grad_bup, small_two,
     ) = call(
-        middle_kernel,
+        functools.partial(middle_kernel, spread_out),
         (
-            shape((rows, width), bf16), shape((width, hidden), bf16), shape((hidden, width), bf16),
-            shape((width, width), bf16), shape((rows, width), f32), shape((rows + stat_rows, lanes), bf16),
+            shape((rows, width), bf16), gradients, gradients, shape((rows, width), f32), shape((rows + stat_rows, lanes), bf16),
             shape(stacked, f32), shape((rows, experts), bf16), shape((experts, width), f32),
             shape((1, hidden), f32), shape((8, width), f32),
         ),
@@ -558,33 +854,106 @@
         tok, cot, heads, gates, picks, lse, normed, w_out, w_up, row(bias_up), w_down, row(bias_down),
         row(gain_two), row(shift_two),
     )
-    grad_up, grad_down, grad_out = lax.psum((grad_up, grad_down, grad_out), ("seq", "row"))
-    do_parts = gather(dom, size)
-    grad_wq, grad_n = call(
-        functools.partial(query_back_kernel, count),
-        (shape((width, width), bf16), shape((rows, width), f32)),
-        [pltpu.VMEM(stacked, bf16), pltpu.VMEM(stacked, bf16), pltpu.VMEM(stacked, f32), pltpu.VMEM((rows, lanes), f32)],
-        40 * mib, 3 * attention_flops,
-        qm, dom, lse, delta, normed, picks, w_query, dlog, route, kvm, *kv_parts,
-    )
-    grad_kv = call(
-        functools.partial(key_back_kernel, count),
-        shape((rows, lanes), bf16),
-        [
-            pltpu.VMEM(stacked, bf16), pltpu.VMEM(stacked, bf16), pltpu.VMEM(stacked, f32),
-            pltpu.VMEM(stacked, f32), pltpu.VMEM((rows, lanes), f32),
-        ],
-        56 * mib, 4 * attention_flops,
-        kvm, *q_parts, *do_parts,
-    )
-    grad_tokens, grad_wkv, small_one = call(
-        final_kernel,
-        (shape((rows, width), f32), shape((width, lanes), f32), shape((8, width), f32)),
-        [], 32 * mib, 4 * rows * width * lanes,
-        tok, normed, grad_n, grad_kv, grad_mid, w_kv, row(gain_one),
-    )
-    grad_wq, grad_wkv, grad_route, grad_bup, small_two, small_one = lax.psum(
-        (grad_wq.astype(f32), grad_wkv, grad_route, grad_bup, small_two, small_one), ("seq", "row")
+    query_flops, key_flops = 3 * attention_flops // 2, 4 * attention_flops // 2
+    results = {}
+    extra_part = shape((width, width // 2), bf16)
+
+    def query_back(parts, first, last, *earlier):
+        finish = (normed, picks, w_query, dlog, route) if last else ()
+        outs = (extra_part, extra_part, shape((rows, width), f32)) if last else ()
+        results["query"] = call(
+            functools.partial(query_back_kernel, spread_out, len(parts), first, last),
+            outs + (shape(stacked, f32),),
+            [pltpu.VMEM(stacked, bf16), pltpu.VMEM(stacked, bf16), pltpu.VMEM((rows, lanes), f32)],
+            40 * mib, query_flops,
+            after(qm, *earlier), dom, lse, delta, kvm, *parts, *(() if first else results["query"]), *finish,
+        )
+        return results["query"][-1]
+
+    def key_back(q_parts, do_parts, first, last, *earlier):
+        results["key"] = call(
+            functools.partial(key_back_kernel, len(q_parts), first, last),
+            ((shape((rows, lanes), bf16),) if last else ()) + state,
+            [pltpu.VMEM(stacked, bf16), pltpu.VMEM(stacked, bf16), pltpu.VMEM((rows, lanes), f32)],
+            56 * mib, key_flops * len(q_parts) * q_parts[0].shape[0] // size,
+            after(kvm, *earlier), *q_parts, *do_parts, *(() if first else results["key"]),
+        )
+        return results["key"][-1]
+
+    extra = 5 + hidden // width + experts
+    small_rows = extra * (width // lanes) + width
+    small_rows = -(-small_rows // 32) * 32
+
+    def finish(*earlier):
+        part = shape((small_rows // 2, lanes), bf16)
+        return call(
+            functools.partial(final_kernel, spread_out),
+            (shape((rows, width), f32), part, part),
+            [pltpu.VMEM((small_rows, lanes), bf16)], 48 * mib, 4 * rows * width * lanes,
+            tok, normed, results["query"][2], after(results["key"][0], *earlier), grad_mid, w_kv, row(gain_one),
+            grad_route, grad_bup, small_two,
+        )
+
+    if spread_out:
+        send, q_near, q_other = lax.optimization_barrier((send, *q_far))
+        q_last = flip_seq(q_other, 2)
+        received = flip_row(send, 1)
+        d_two = jnp.stack([dom, flip_seq(dom, 1)])
+        received = after(received, query_back(near, True, False))
+        part = shape((keep.shape[0] // 2, width // 2), bf16)
+        one, one_send, two, two_send = simple(after_core_kernel, (part,) * 4, keep, received)
+        one_in, two_in = flip_row(one_send, 2), flip_seq(two_send, 1)
+        d_near, d_other = flip_seq(d_two, 2), flip_seq(d_two, 4)
+        query_back(others, False, True, one)
+        extra_keep, extra_send = results["query"][:2]
+        part = shape((width // 2, width // 2), bf16)
+        extra_keep, extra_send = simple(split_x_kernel, (part,) * 2, extra_keep, flip_row(extra_send, 1))
+        extra_in = flip_row(extra_send, 2)
+        done = key_back([q_two], [d_two], True, False, extra_keep)
+        wider = shape((keep.shape[0] // 4 + width // 4, width // 2), bf16)
+        part = shape((keep.shape[0] // 4, width // 2), bf16)
+        one, one_send, two, two_send = simple(
+            after_first_kernel, (wider, wider, part, part), one, after(one_in, done), two, two_in, extra_keep, extra_in
+        )
+        one_in, two_in = flip_seq(one_send, 1), flip_row(two_send, 2)
+        d_last = flip_seq(d_other, 2)
+        done = key_back([q_near, q_other], [d_near, d_other], False, False, one)
+        piece += width // parts_of
+        part = shape((piece, width), bf16)
+        sent = simple(after_second_kernel, (part,) * 4, one, after(one_in, done), two, two_in)
+        planes = [flip_seq(sent[i], 2 * i) for i in (1, 2, 3)]
+        done = key_back([q_last], [d_last], False, True, sent[0])
+        mine = simple(sum_kernel, part, after(sent[0], done), *planes)
+        arrived = [flip_seq(mine, 2 * i) for i in (1, 2, 3)]
+        grad_tokens, *small = finish(mine)
+        large, small = finish_sums((mine, arrived), small)
+    else:
+        query_back(all_kv, True, True)
+        gathered = [lax.all_gather(m, "seq", axis=0, tiled=False) for m in (qm, dom)]
+        key_back(gathered[:1], gathered[1:], True, True)
+        grad_tokens, *small = finish()
+        small = lax.psum(small, ("seq", "row"))
+        sums = lax.psum((keep, send, *results["query"][:2]), ("seq", "row"))
+        large = ()
+        for total, more in zip(sums[:2], sums[2:]):
+            more = more.reshape(16, 2, -1, width // 2).transpose(0, 2, 1, 3).reshape(16, -1, width)
+            cube = jnp.concatenate([total.reshape(16, piece, width), more], axis=1)
+            cube = cube.reshape((4, 2, 2) + cube.shape[1:])
+            for x in (0, 1):
+                large += (cube[:, :, x, :, : width // 2].transpose(1, 0, 2, 3).reshape(-1, width // 2),)
+            for y in (0, 1):
+                large += (cube[:, y, :, :, width // 2 :].transpose(1, 0, 2, 3).reshape(-1, width // 2),)
+    grad_wkv, grad_route, grad_bup, grad_small = call(
+        functools.partial(unpack_small_kernel, spread_out),
+        (
+            shape((width, lanes), f32), shape((experts, width), f32), shape((1, hidden), f32), shape((8, width), f32),
+        ),
+        [pltpu.VMEM((small_rows, lanes), f32)], 48 * mib, 0, *small,
+    )
+    grad_up, grad_down, grad_out, grad_wq = call(
+        functools.partial(unpack_kernel, spread_out),
+        (shape((width, hidden), f32), shape((hidden, width), f32)) + (shape((width, width), f32),) * 2,
+        [], 48 * mib, 0, *large,
     )
     return (
         layer_out[None],
@@ -592,15 +961,15 @@
         grad_wq,
         grad_wkv,
         grad_route.T,
-        grad_out.astype(f32),
-        grad_up.astype(f32),
+        grad_out,
+        grad_up,
         grad_bup.reshape(-1),
-        grad_down.astype(f32),
-        small_two[0],
-        small_one[0],
-        small_one[1],
-        small_two[1],
-        small_two[2],
+        grad_down,
+        grad_small[2],
+        grad_small[0],
+        grad_small[1],
+        grad_small[3],
+        grad_small[4],
     )
 
 

time: 441 us -> 238 us (0.54); the launches traced: 433 us -> 236 us
  waiting for transfers between devices: 196 us -> 44.8 us
  blocking collectives: 85.6 us -> 0 us
  Pallas kernels: 54.1 us -> 112 us
  between operations: 14.8 us -> 1.43 us
  other arithmetic: 7.99 us -> 0.19 us
  starting transfers between devices: 55.6 us -> 61.6 us
    psum x2 -> x0, waiting for transfers between devices: 134 us -> none  [the longest x1 122 us: local(): lax.psum((grad_wq.astype(f32), grad_wkv, grad_route, grad_bup, small_two,...]
    psum x1 -> x0, blocking collectives: 85.6 us -> none  [local(): lax.psum((grad_wq.astype(f32), grad_wkv, grad_route, grad_bup, small_two,...]
    pallas_call x6 -> x18, Pallas kernels: 54.1 us -> 112 us  [call(): pl.pallas_call(kernel, out_shape=out_shape, in_specs=[whole] * len(operan...]
    ppermute x21 -> x42, waiting for transfers between devices: 62 us -> 44.8 us  [the longest x28 36.2 us: flip_seq(): return lax.ppermute(x, 'seq', [(i, i ^ mask) for i in range(8)])]
    convert_element_type x3 -> x5, other arithmetic: 7.99 us -> 0.12 us  [add(): return (a.astype(f32) + b.astype(f32)).astype(bf16)]
    ppermute x21 -> x42, starting transfers between devices: 55.5 us -> 61.6 us  [the longest x28 47.2 us: flip_seq(): return lax.ppermute(x, 'seq', [(i, i ^ mask) for i in range(8)])]
    unnamed x95 -> x88, local copies, waits for them, and re-layouts: 18.1 us -> 15.8 us
  transfers between devices with their start and end apart: 23 -> 42, of which waited for: 12 -> 14; matrix products, arithmetic and copies ran while one was open for 2% -> 0% of each run, Pallas kernels for 5% -> 43%
where the time goes in v2:
time: 238 us; the launch traced here: 236 us
  Pallas kernels  112 us (47%)
  starting transfers between devices  61.6 us (26%)
  waiting for transfers between devices  44.8 us (19%)
  local copies, waits for them, and re-layouts  16.5 us (7%)
    pallas_call x18, Pallas kernels, call(): pl.pallas_call(kernel, out_shape=out_shape, in_specs=[whole] * len(operan...  112 us
    ppermute x28, starting transfers between devices, flip_seq(): return lax.ppermute(x, 'seq', [(i, i ^ mask) for i in range(8)])  47.2 us
    ppermute x28, waiting for transfers between devices, flip_seq(): return lax.ppermute(x, 'seq', [(i, i ^ mask) for i in range(8)])  36.2 us
    unnamed x88, local copies, waits for them, and re-layouts  15.8 us
    ppermute x14, starting transfers between devices, flip_row(): return lax.ppermute(x, 'row', [(i, i ^ mask) for i in range(4)])  14.3 us
    ppermute x14, waiting for transfers between devices, flip_row(): return lax.ppermute(x, 'row', [(i, i ^ mask) for i in range(4)])  8.58 us
  transfers between devices with their start and end apart: 42, of which 14 were waited for; matrix products, arithmetic and copies ran while one was open for 0% of the time, Pallas kernels for 43%

profile of v2, /device:TPU:0, one launch (start us, length us, event | category | flops | bytes accessed | tf_op | source)
XLA Modules:
  0.0 236.1 jit_solution(11065133024168189017)
XLA Ops:
  11.0 4.0 %collective-permute-start.2 = (bf16[656,128]{1,0:T(8,128)(2,1)S(1)}, bf16[656,128]{1,0:T(8,128)(2,1)S(1)}, u32[]{:S(2)}, u32[]{:S(2)}) collective-permute-start(bf16[656,128]{1,0:T(8,128)(2,1)S(1)} %get-tuple-element.129.own), channel_id=1, source_target_pairs={{0,16},{4,20},{8,24},{12,28},{16,0},{20,4},{24,8},{28,12},{1,17},{... | collective-permute-start | bytes 503816 | tf_op jit(solution)/shard_map/ppermute | solution.py:706
  19.8 4.7 %collective-permute-done.2 = bf16[656,128]{1,0:T(8,128)(2,1)S(1)} collective-permute-done((bf16[656,128]{1,0:T(8,128)(2,1)S(1)}, bf16[656,128]{1,0:T(8,128)(2,1)S(1)}, u32[]{:S(2)}, u32[]{:S(2)}) %collective-permute-start.2) | collective-permute-done | bytes 167968 | tf_op jit(solution)/shard_map/ppermute | solution.py:706
  27.4 3.1 %collective-permute-done.6 = bf16[656,128]{1,0:T(8,128)(2,1)S(1)} collective-permute-done((bf16[656,128]{1,0:T(8,128)(2,1)S(1)}, bf16[656,128]{1,0:T(8,128)(2,1)S(1)}, u32[]{:S(2)}, u32[]{:S(2)}) %collective-permute-start.6) | collective-permute-done | bytes 167968 | tf_op jit(solution)/shard_map/ppermute | solution.py:706
  30.5 12.1 %shard_map.264 = (f32[1280,128]{1,0:T(8,128)S(1)}, f32[1280,128]{1,0:T(8,128)S(1)}) custom-call(bf16[656,128]{1,0:T(8,128)(2,1)S(1)} %get-tuple-element.105.qm, bf16[656,128]{1,0:T(8,128)(2,1)S(1)} %get-tuple-element.129.own, bf16[1,656,128]{2,1,0:T(8,128)(2,1)S(1)} %bitcast.40, bf16[1,656,128]{2,1,0:T(8,128)(2,1)S(1)} %bitcast.54, ...), custom_call_target="tpu_custom_call" | custom-call | flops 1677721600 | bytes 1007616 | tf_op jit(solution)/shard_map/pallas_call | solution.py:767
  42.9 7.8 %shard_map.265 = (f32[640,128]{1,0:T(8,128)S(1)}, f32[1280,128]{1,0:T(8,128)S(1)}, f32[1280,128]{1,0:T(8,128)}, f32[1280,128]{1,0:T(8,128)}) custom-call(bf16[656,128]{1,0:T(8,128)(2,1)S(1)} %get-tuple-element.105.qm, bf16[656,128]{1,0:T(8,128)(2,1)S(1)} %get-tuple-element.129.own, bf16[1,656,128]{2,1,0:T(8,128)(2,1)S(1)} %bitcast.52, ...), custom_call_target="tpu_custom_call" | custom-call | flops 1677721600 | bytes 2318336 | tf_op jit(solution)/shard_map/pallas_call | solution.py:767
  52.2 22.3 %shard_map.266 = (bf16[640,512]{1,0:T(8,128)(2,1)}, bf16[2304,512]{1,0:T(8,128)(2,1)}, bf16[2304,512]{1,0:T(8,128)(2,1)}, f32[640,512]{1,0:T(8,128)}, bf16[720,1...) custom-call(bf16[640,512]{1,0:T(8,128)(2,1)} %bitcast.33, ...), custom_call_target="tpu_custom_call" | custom-call | flops 8053063680 | bytes 8665088 | tf_op jit(solution)/shard_map/pallas_call | solution.py:767
  78.7 22.7 %shard_map.267.rest_4_ = f32[1280,128]{1,0:T(8,128)S(1)} custom-call(bf16[656,128]{1,0:T(8,128)(2,1)S(1)} %get-tuple-element.105.qm, bf16[720,128]{1,0:T(8,128)(2,1)S(1)} %copy-done.6, f32[1280,128]{1,0:T(8,128)S(1)} %copy-done.28, f32[1280,128]{1,0:T(8,128)S(1)} %copy-done.29, bf16[656,128]{1,0:T(8,128)(2,1)S(1)} %get-tuple-element.129.own, ...), custom_call_target="tpu_custom_call" | custom-call | flops 2516582400 | bytes 2502656 | tf_op jit(solution)/shard_map/pallas_call | solution.py:767
  105.2 4.8 %collective-permute-start.11 = (bf16[1152,256]{1,0:T(8,128)(2,1)S(1)}, bf16[1152,256]{1,0:T(8,128)(2,1)S(1)}, u32[]{:S(2)}, u32[]{:S(2)}) collective-permute-start(bf16[1152,256]{1,0:T(8,128)(2,1)S(1)} %get-tuple-element.108), channel_id=1, source_target_pairs={{0,2},{1,3},{2,0},{3,1},{4,6},{5,7},{6,4},{7,5},{8,10},{9,11},{10,... | collective-permute-start | bytes 1769480 | tf_op jit(solution)/shard_map/ppermute | solution.py:702
  110.3 8.2 %shard_map.269 = (bf16[512,256]{1,0:T(8,128)(2,1)S(1)}, bf16[512,256]{1,0:T(8,128)(2,1)S(1)}, f32[640,512]{1,0:T(8,128)S(1)}, f32[1280,128]{1,0:T(8,128)}) custom-call(bf16[656,128]{1,0:T(8,128)(2,1)S(1)} %get-tuple-element.105.qm, bf16[720,128]{1,0:T(8,128)(2,1)S(1)} %copy-done.7, f32[1280,128]{1,0:T(8,128)S(1)} %copy-done.28, f32[1280,128]{1,0:T(8,128)S(1)} %copy-done.30, ...), custom_call_target="tpu_custom_call" | custom-call | flops 2516582400 | bytes 5011456 | tf_op jit(solution)/shard_map/pallas_call | solution.py:767
  118.6 8.0 %collective-permute-start.18 = (bf16[2,720,128]{2,1,0:T(8,128)(2,1)S(1)}, bf16[2,720,128]{2,1,0:T(8,128)(2,1)S(1)}, u32[]{:S(2)}, u32[]{:S(2)}) collective-permute-start(bf16[2,720,128]{2,1,0:T(8,128)(2,1)S(1)} %pad_maximum_fusion.rest_1_), channel_id=1, source_target_pairs={{0,16},{4,20},{8,24},{12,28},{16,0},{20,4},{24,8},{28,12},{1,17},{... | collective-permute-start | bytes 1105928 | tf_op jit(solution)/shard_map/ppermute | solution.py:706
  126.7 3.5 %collective-permute-start.15 = (bf16[256,256]{1,0:T(8,128)(2,1)S(1)}, bf16[256,256]{1,0:T(8,128)(2,1)S(1)}, u32[]{:S(2)}, u32[]{:S(2)}) collective-permute-start(bf16[256,256]{1,0:T(8,128)(2,1)S(1)} %get-tuple-element.117), channel_id=1, source_target_pairs={{0,2},{1,3},{2,0},{3,1},{4,6},{5,7},{6,4},{7,5},{8,10},{9,11},{10,... | collective-permute-start | bytes 393224 | tf_op jit(solution)/shard_map/ppermute | solution.py:702
  130.2 8.1 %shard_map.271 = (f32[1280,128]{1,0:T(8,128)}, f32[1280,128]{1,0:T(8,128)}) custom-call(bf16[656,128]{1,0:T(8,128)(2,1)} %copy-done.18, bf16[2,656,128]{2,1,0:T(8,128)(2,1)} %copy-done.35, bf16[2,720,128]{2,1,0:T(8,128)(2,1)} %copy-done.34), custom_call_target="tpu_custom_call" | custom-call | flops 838860800 | bytes 872448 | tf_op jit(solution)/shard_map/pallas_call | solution.py:767
  146.7 14.2 %shard_map.273 = (f32[1280,128]{1,0:T(8,128)}, f32[1280,128]{1,0:T(8,128)}) custom-call(bf16[656,128]{1,0:T(8,128)(2,1)} %copy-done.18, bf16[2,656,128]{2,1,0:T(8,128)(2,1)} %copy-done.41, bf16[2,656,128]{2,1,0:T(8,128)(2,1)} %copy-done.39, bf16[2,720,128]{2,1,0:T(8,128)(2,1)} %copy-done.37, bf16[2,720,128]{2,1,0:T(8,128)(2,1)} %copy-done.36, ...), custom_call_target="tpu_custom_call" | custom-call | flops 1677721600 | bytes 2887680 | tf_op jit(solution)/shard_map/pallas_call | solution.py:767
  161.4 4.3 %collective-permute-start.24 = (bf16[160,512]{1,0:T(8,128)(2,1)S(1)}, bf16[160,512]{1,0:T(8,128)(2,1)S(1)}, u32[]{:S(2)}, u32[]{:S(2)}) collective-permute-start(bf16[160,512]{1,0:T(8,128)(2,1)S(1)} %get-tuple-element.134), channel_id=1, source_target_pairs={{0,24},{4,28},{8,16},{12,20},{16,8},{20,12},{24,0},{28,4},{1,25},{... | collective-permute-start | bytes 491528 | tf_op jit(solution)/shard_map/ppermute | solution.py:706
  166.5 3.3 %shard_map.275 = (bf16[640,128]{1,0:T(8,128)(2,1)}, f32[1280,128]{1,0:T(8,128)}, f32[1280,128]{1,0:T(8,128)}) custom-call(bf16[656,128]{1,0:T(8,128)(2,1)} %copy-done.18, bf16[2,656,128]{2,1,0:T(8,128)(2,1)} %copy-done.42, bf16[2,720,128]{2,1,0:T(8,128)(2,1)} %copy-done.38, f32[1280,128]{1,0:T(8,128)} %get-tuple-element.130.rest_2_, ...), custom_call_target="tpu_custom_call" | custom-call | flops 838860800 | bytes 2183168 | tf_op jit(solution)/shard_map/pallas_call | solution.py:767
  169.8 5.0 %collective-permute-done.23.refs_2_ = bf16[160,512]{1,0:T(8,128)(2,1)S(1)} collective-permute-done((bf16[160,512]{1,0:T(8,128)(2,1)S(1)}, bf16[160,512]{1,0:T(8,128)(2,1)S(1)}, u32[]{:S(2)}, u32[]{:S(2)}) %collective-permute-start.23) | collective-permute-done | bytes 163872 | tf_op jit(solution)/shard_map/ppermute | solution.py:706
  179.5 3.0 %collective-permute-start.27 = (bf16[304,128]{1,0:T(8,128)(2,1)S(1)}, bf16[304,128]{1,0:T(8,128)(2,1)S(1)}, u32[]{:S(2)}, u32[]{:S(2)}) collective-permute-start(bf16[304,128]{1,0:T(8,128)(2,1)S(1)} %add_convert_fusion.4), channel_id=1, source_target_pairs={{0,2},{1,3},{2,0},{3,1},{4,6},{5,7},{6,4},{7,5},{8,10},{9,11},{10,... | collective-permute-start | bytes 233480 | tf_op jit(solution)/shard_map/ppermute | solution.py:702
  191.5 8.3 %collective-permute-done.28.refs_2_ = bf16[160,512]{1,0:T(8,128)(2,1)S(1)} collective-permute-done((bf16[160,512]{1,0:T(8,128)(2,1)S(1)}, bf16[160,512]{1,0:T(8,128)(2,1)S(1)}, u32[]{:S(2)}, u32[]{:S(2)}) %collective-permute-start.28) | collective-permute-done | bytes 163872 | tf_op jit(solution)/shard_map/ppermute | solution.py:706
  202.7 3.1 %collective-permute-start.33 = (bf16[304,128]{1,0:T(8,128)(2,1)S(1)}, bf16[304,128]{1,0:T(8,128)(2,1)S(1)}, u32[]{:S(2)}, u32[]{:S(2)}) collective-permute-start(bf16[304,128]{1,0:T(8,128)(2,1)S(1)} %add_convert_fusion.2), channel_id=1, source_target_pairs={{0,8},{4,12},{8,0},{12,4},{16,24},{20,28},{24,16},{28,20},{1,9},{5... | collective-permute-start | bytes 233480 | tf_op jit(solution)/shard_map/ppermute | solution.py:706
  208.7 3.1 %collective-permute-done.37 = bf16[640,256]{1,0:T(8,128)(2,1)S(1)} collective-permute-done((bf16[640,256]{1,0:T(8,128)(2,1)S(1)}, bf16[640,256]{1,0:T(8,128)(2,1)S(1)}, u32[]{:S(2)}, u32[]{:S(2)}) %collective-permute-start.37) | collective-permute-done | bytes 327712 | tf_op jit(solution)/shard_map/ppermute | solution.py:702
  212.0 4.1 %collective-permute-start.34 = (bf16[304,128]{1,0:T(8,128)(2,1)S(1)}, bf16[304,128]{1,0:T(8,128)(2,1)S(1)}, u32[]{:S(2)}, u32[]{:S(2)}) collective-permute-start(bf16[304,128]{1,0:T(8,128)(2,1)S(1)} %add_convert_fusion.1), channel_id=1, source_target_pairs={{0,16},{4,20},{8,24},{12,28},{16,0},{20,4},{24,8},{28,12},{1,17},{... | collective-permute-start | bytes 233480 | tf_op jit(solution)/shard_map/ppermute | solution.py:706
  216.1 4.0 %collective-permute-done.34 = bf16[304,128]{1,0:T(8,128)(2,1)S(1)} collective-permute-done((bf16[304,128]{1,0:T(8,128)(2,1)S(1)}, bf16[304,128]{1,0:T(8,128)(2,1)S(1)}, u32[]{:S(2)}, u32[]{:S(2)}) %collective-permute-start.34) | collective-permute-done | bytes 77856 | tf_op jit(solution)/shard_map/ppermute | solution.py:706
  223.7 5.4 %collective-permute-done.39.refs_3_ = bf16[1280,256]{1,0:T(8,128)(2,1)S(1)} collective-permute-done((bf16[1280,256]{1,0:T(8,128)(2,1)S(1)}, bf16[1280,256]{1,0:T(8,128)(2,1)S(1)}, u32[]{:S(2)}, u32[]{:S(2)}) %collective-permute-start.39) | collective-permute-done | bytes 655392 | tf_op jit(solution)/shard_map/ppermute | solution.py:706
  231.2 4.7 %shard_map.279 = (f32[512,2048]{1,0:T(8,128)}, f32[2048,512]{1,0:T(8,128)}, f32[512,512]{1,0:T(8,128)}, f32[512,512]{1,0:T(8,128)}) custom-call(bf16[1280,256]{1,0:T(8,128)(2,1)S(1)} %constant_dynamic-update-slice_fusion.refs_0_, bf16[1280,256]{1,0:T(8,128)(2,1)S(1)} %collective-permute-done.32.refs_1_, ...), custom_call_target="tpu_custom_call" | custom-call | bytes 5242880 | tf_op jit(solution)/shard_map/pallas_call | solution.py:767
  (176 shorter events, 62.7 us)
Async XLA Ops:
  11.0 13.6 %collective-permute-start.2 = (bf16[656,128]{1,0:T(8,128)(2,1)S(1)}, bf16[656,128]{1,0:T(8,128)(2,1)S(1)}, u32[]{:S(2)}, u32[]{:S(2)}) collective-permute-start(bf16[656,128]{1,0:T(8,128)(2,1)S(1)} %get-tuple-element.129.own), channel_id=1, source_target_pairs={{0,16},{4,20},{8,24},{12,28},{16,0},{20,4},{24,8},{28,12},{1,17},{... | collective-permute-start | bytes 503816 | tf_op jit(solution)/shard_map/ppermute | solution.py:706
  18.6 24.1 %collective-permute-start.5 = (bf16[656,128]{1,0:T(8,128)(2,1)S(1)}, bf16[656,128]{1,0:T(8,128)(2,1)S(1)}, u32[]{:S(2)}, u32[]{:S(2)}) collective-permute-start(bf16[656,128]{1,0:T(8,128)(2,1)S(1)} %get-tuple-element.129.own), channel_id=1, source_target_pairs={{0,28},{4,24},{8,20},{12,16},{16,12},{20,8},{24,4},{28,0},{1,29},{... | collective-permute-start | bytes 503816 | tf_op jit(solution)/shard_map/ppermute | solution.py:706
  24.5 18.3 %collective-permute-start.3 = (bf16[656,128]{1,0:T(8,128)(2,1)S(1)}, bf16[656,128]{1,0:T(8,128)(2,1)S(1)}, u32[]{:S(2)}, u32[]{:S(2)}) collective-permute-start(bf16[656,128]{1,0:T(8,128)(2,1)S(1)} %collective-permute-done.2), channel_id=1, source_target_pairs={{0,4},{4,0},{8,12},{12,8},{16,20},{20,16},{24,28},{28,24},{1,5},{5... | collective-permute-start | bytes 503816 | tf_op jit(solution)/shard_map/ppermute | solution.py:706
  26.7 16.1 %collective-permute-start.4 = (bf16[656,128]{1,0:T(8,128)(2,1)S(1)}, bf16[656,128]{1,0:T(8,128)(2,1)S(1)}, u32[]{:S(2)}, u32[]{:S(2)}) collective-permute-start(bf16[656,128]{1,0:T(8,128)(2,1)S(1)} %collective-permute-done.2), channel_id=1, source_target_pairs={{0,8},{4,12},{8,0},{12,4},{16,24},{20,28},{24,16},{28,20},{1,9},{5... | collective-permute-start | bytes 503816 | tf_op jit(solution)/shard_map/ppermute | solution.py:706
  26.7 16.1 %collective-permute-start.1 = (bf16[656,128]{1,0:T(8,128)(2,1)S(1)}, bf16[656,128]{1,0:T(8,128)(2,1)S(1)}, u32[]{:S(2)}, u32[]{:S(2)}) collective-permute-start(bf16[656,128]{1,0:T(8,128)(2,1)S(1)} %collective-permute-done), channel_id=1, source_target_pairs={{0,4},{4,0},{8,12},{12,8},{16,20},{20,16},{24,28},{28,24},{1,5},{5... | collective-permute-start | bytes 503816 | tf_op jit(solution)/shard_map/ppermute | solution.py:706
  42.6 31.8 %collective-permute-start.8 = (bf16[2,656,128]{2,1,0:T(8,128)(2,1)S(1)}, bf16[2,656,128]{2,1,0:T(8,128)(2,1)S(1)}, u32[]{:S(2)}, u32[]{:S(2)}) collective-permute-start(bf16[2,656,128]{2,1,0:T(8,128)(2,1)S(1)} %pad_maximum_fusion.1.rest_0_), channel_id=1, source_target_pairs={{0,8},{4,12},{8,0},{12,4},{16,24},{20,28},{24,16},{28,20},{1,9},{5... | collective-permute-start | bytes 1007624 | tf_op jit(solution)/shard_map/ppermute | solution.py:706
  42.7 31.7 %collective-permute-start.9 = (bf16[2,656,128]{2,1,0:T(8,128)(2,1)S(1)}, bf16[2,656,128]{2,1,0:T(8,128)(2,1)S(1)}, u32[]{:S(2)}, u32[]{:S(2)}) collective-permute-start(bf16[2,656,128]{2,1,0:T(8,128)(2,1)S(1)} %pad_maximum_fusion.1.rest_0_), channel_id=1, source_target_pairs={{0,16},{4,20},{8,24},{12,28},{16,0},{20,4},{24,8},{28,12},{1,17},{... | collective-permute-start | bytes 1007624 | tf_op jit(solution)/shard_map/ppermute | solution.py:706
  74.5 26.9 %collective-permute-start.10 = (bf16[2304,512]{1,0:T(8,128)(2,1)}, bf16[2304,512]{1,0:T(8,128)(2,1)S(1)}, u32[]{:S(2)}, u32[]{:S(2)}) collective-permute-start(bf16[2304,512]{1,0:T(8,128)(2,1)} %get-tuple-element.100), channel_id=1, source_target_pairs={{0,1},{1,0},{2,3},{3,2},{4,5},{5,4},{6,7},{7,6},{8,9},{9,8},{10,11... | collective-permute-start | bytes 7077896 | tf_op jit(solution)/shard_map/ppermute | solution.py:702
  74.6 44.0 %collective-permute-start.13 = (bf16[720,128]{1,0:T(8,128)(2,1)}, bf16[720,128]{1,0:T(8,128)(2,1)S(1)}, u32[]{:S(2)}, u32[]{:S(2)}) collective-permute-start(bf16[720,128]{1,0:T(8,128)(2,1)} %get-tuple-element.101.dom), channel_id=1, source_target_pairs={{0,4},{4,0},{8,12},{12,8},{16,20},{20,16},{24,28},{28,24},{1,5},{5... | collective-permute-start | bytes 552968 | tf_op jit(solution)/shard_map/ppermute | solution.py:706
  105.2 33.1 %collective-permute-start.11 = (bf16[1152,256]{1,0:T(8,128)(2,1)S(1)}, bf16[1152,256]{1,0:T(8,128)(2,1)S(1)}, u32[]{:S(2)}, u32[]{:S(2)}) collective-permute-start(bf16[1152,256]{1,0:T(8,128)(2,1)S(1)} %get-tuple-element.108), channel_id=1, source_target_pairs={{0,2},{1,3},{2,0},{3,1},{4,6},{5,7},{6,4},{7,5},{8,10},{9,11},{10,... | collective-permute-start | bytes 1769480 | tf_op jit(solution)/shard_map/ppermute | solution.py:702
  110.1 28.3 %collective-permute-start.14 = (bf16[1152,256]{1,0:T(8,128)(2,1)S(1)}, bf16[1152,256]{1,0:T(8,128)(2,1)S(1)}, u32[]{:S(2)}, u32[]{:S(2)}) collective-permute-start(bf16[1152,256]{1,0:T(8,128)(2,1)S(1)} %get-tuple-element.116), channel_id=1, source_target_pairs={{0,4},{4,0},{8,12},{12,8},{16,20},{20,16},{24,28},{28,24},{1,5},{5... | collective-permute-start | bytes 1769480 | tf_op jit(solution)/shard_map/ppermute | solution.py:706
  118.6 25.3 %collective-permute-start.18 = (bf16[2,720,128]{2,1,0:T(8,128)(2,1)S(1)}, bf16[2,720,128]{2,1,0:T(8,128)(2,1)S(1)}, u32[]{:S(2)}, u32[]{:S(2)}) collective-permute-start(bf16[2,720,128]{2,1,0:T(8,128)(2,1)S(1)} %pad_maximum_fusion.rest_1_), channel_id=1, source_target_pairs={{0,16},{4,20},{8,24},{12,28},{16,0},{20,4},{24,8},{28,12},{1,17},{... | collective-permute-start | bytes 1105928 | tf_op jit(solution)/shard_map/ppermute | solution.py:706
  126.6 19.3 %collective-permute-start.17 = (bf16[2,720,128]{2,1,0:T(8,128)(2,1)S(1)}, bf16[2,720,128]{2,1,0:T(8,128)(2,1)S(1)}, u32[]{:S(2)}, u32[]{:S(2)}) collective-permute-start(bf16[2,720,128]{2,1,0:T(8,128)(2,1)S(1)} %pad_maximum_fusion.rest_1_), channel_id=1, source_target_pairs={{0,8},{4,12},{8,0},{12,4},{16,24},{20,28},{24,16},{28,20},{1,9},{5... | collective-permute-start | bytes 1105928 | tf_op jit(solution)/shard_map/ppermute | solution.py:706
  138.7 22.3 %collective-permute-start.16 = (bf16[704,256]{1,0:T(8,128)(2,1)S(1)}, bf16[704,256]{1,0:T(8,128)(2,1)S(1)}, u32[]{:S(2)}, u32[]{:S(2)}) collective-permute-start(bf16[704,256]{1,0:T(8,128)(2,1)S(1)} %get-tuple-element.119), channel_id=1, source_target_pairs={{0,4},{4,0},{8,12},{12,8},{16,20},{20,16},{24,28},{28,24},{1,5},{5... | collective-permute-start | bytes 1081352 | tf_op jit(solution)/shard_map/ppermute | solution.py:706
  140.1 20.9 %collective-permute-start.19 = (bf16[576,256]{1,0:T(8,128)(2,1)S(1)}, bf16[576,256]{1,0:T(8,128)(2,1)S(1)}, u32[]{:S(2)}, u32[]{:S(2)}) collective-permute-start(bf16[576,256]{1,0:T(8,128)(2,1)S(1)} %get-tuple-element.127), channel_id=1, source_target_pairs={{0,2},{1,3},{2,0},{3,1},{4,6},{5,7},{6,4},{7,5},{8,10},{9,11},{10,... | collective-permute-start | bytes 884744 | tf_op jit(solution)/shard_map/ppermute | solution.py:702
  143.9 21.8 %collective-permute-start.21 = (bf16[2,720,128]{2,1,0:T(8,128)(2,1)S(1)}, bf16[2,720,128]{2,1,0:T(8,128)(2,1)S(1)}, u32[]{:S(2)}, u32[]{:S(2)}) collective-permute-start(bf16[2,720,128]{2,1,0:T(8,128)(2,1)S(1)} %collective-permute-done.18.rest_3_), channel_id=1, source_target_pairs={{0,8},{4,12},{8,0},{12,4},{16,24},{20,28},{24,16},{28,20},{1,9},{5... | collective-permute-start | bytes 1105928 | tf_op jit(solution)/shard_map/ppermute | solution.py:706
  144.1 21.6 %collective-permute-start.20 = (bf16[2,656,128]{2,1,0:T(8,128)(2,1)S(1)}, bf16[2,656,128]{2,1,0:T(8,128)(2,1)S(1)}, u32[]{:S(2)}, u32[]{:S(2)}) collective-permute-start(bf16[2,656,128]{2,1,0:T(8,128)(2,1)S(1)} %copy-done.40), channel_id=1, source_target_pairs={{0,8},{4,12},{8,0},{12,4},{16,24},{20,28},{24,16},{28,20},{1,9},{5... | collective-permute-start | bytes 1007624 | tf_op jit(solution)/shard_map/ppermute | solution.py:706
  161.3 13.5 %collective-permute-start.23 = (bf16[160,512]{1,0:T(8,128)(2,1)S(1)}, bf16[160,512]{1,0:T(8,128)(2,1)S(1)}, u32[]{:S(2)}, u32[]{:S(2)}) collective-permute-start(bf16[160,512]{1,0:T(8,128)(2,1)S(1)} %get-tuple-element.133), channel_id=1, source_target_pairs={{0,16},{4,20},{8,24},{12,28},{16,0},{20,4},{24,8},{28,12},{1,17},{... | collective-permute-start | bytes 491528 | tf_op jit(solution)/shard_map/ppermute | solution.py:706
  184.8 15.0 %collective-permute-start.28 = (bf16[160,512]{1,0:T(8,128)(2,1)S(1)}, bf16[160,512]{1,0:T(8,128)(2,1)S(1)}, u32[]{:S(2)}, u32[]{:S(2)}) collective-permute-start(bf16[160,512]{1,0:T(8,128)(2,1)S(1)} %shard_map.276.refs_0_), channel_id=1, source_target_pairs={{0,16},{4,20},{8,24},{12,28},{16,0},{20,4},{24,8},{28,12},{1,17},{... | collective-permute-start | bytes 491528 | tf_op jit(solution)/shard_map/ppermute | solution.py:706
  185.8 14.1 %collective-permute-start.29 = (bf16[160,512]{1,0:T(8,128)(2,1)S(1)}, bf16[160,512]{1,0:T(8,128)(2,1)S(1)}, u32[]{:S(2)}, u32[]{:S(2)}) collective-permute-start(bf16[160,512]{1,0:T(8,128)(2,1)S(1)} %shard_map.276.refs_0_), channel_id=1, source_target_pairs={{0,24},{4,28},{8,16},{12,20},{16,8},{20,12},{24,0},{28,4},{1,25},{... | collective-permute-start | bytes 491528 | tf_op jit(solution)/shard_map/ppermute | solution.py:706
  187.2 15.4 %collective-permute-start.31 = (bf16[304,128]{1,0:T(8,128)(2,1)S(1)}, bf16[304,128]{1,0:T(8,128)(2,1)S(1)}, u32[]{:S(2)}, u32[]{:S(2)}) collective-permute-start(bf16[304,128]{1,0:T(8,128)(2,1)S(1)} %add_convert_fusion.3), channel_id=1, source_target_pairs={{0,4},{4,0},{8,12},{12,8},{16,20},{20,16},{24,28},{28,24},{1,5},{5... | collective-permute-start | bytes 233480 | tf_op jit(solution)/shard_map/ppermute | solution.py:706
  207.9 15.8 %collective-permute-start.32 = (bf16[1280,256]{1,0:T(8,128)(2,1)S(1)}, bf16[1280,256]{1,0:T(8,128)(2,1)S(1)}, u32[]{:S(2)}, u32[]{:S(2)}) collective-permute-start(bf16[1280,256]{1,0:T(8,128)(2,1)S(1)} %constant_dynamic-update-slice_fusion.refs_0_), channel_id=1, source_target_pairs={{0,2},{1,3},{2,0},{3,1},{4,6},{5,7},{6,4},{7,5},{8,10},{9,11},{10,... | collective-permute-start | bytes 1966088 | tf_op jit(solution)/shard_map/ppermute | solution.py:702
  208.7 15.0 %collective-permute-start.36 = (bf16[1280,256]{1,0:T(8,128)(2,1)S(1)}, bf16[1280,256]{1,0:T(8,128)(2,1)S(1)}, u32[]{:S(2)}, u32[]{:S(2)}) collective-permute-start(bf16[1280,256]{1,0:T(8,128)(2,1)S(1)} %constant_dynamic-update-slice_fusion.refs_0_), channel_id=1, source_target_pairs={{0,1},{1,0},{2,3},{3,2},{4,5},{5,4},{6,7},{7,6},{8,9},{9,8},{10,11... | collective-permute-start | bytes 1966088 | tf_op jit(solution)/shard_map/ppermute | solution.py:702
  211.9 17.1 %collective-permute-start.39 = (bf16[1280,256]{1,0:T(8,128)(2,1)S(1)}, bf16[1280,256]{1,0:T(8,128)(2,1)S(1)}, u32[]{:S(2)}, u32[]{:S(2)}) collective-permute-start(bf16[1280,256]{1,0:T(8,128)(2,1)S(1)} %constant_dynamic-update-slice_fusion.2.refs_2_), channel_id=1, source_target_pairs={{0,4},{4,0},{8,12},{12,8},{16,20},{20,16},{24,28},{28,24},{1,5},{5... | collective-permute-start | bytes 1966088 | tf_op jit(solution)/shard_map/ppermute | solution.py:706
  (61 other events, 581.4 us)
